TPU v7x, 256 devices: a whole 4x4x8 slice. The times are simulated.
256 devices in a mesh: mode: 8 (over z_hi, core), space: 32 (over z_lo, y, x).
Axes of the slice: x: 4, y: 4, z: 8 (z_hi: 4, z_lo: 2; z = z_hi * 2 + z_lo), core: 2. Of those that a mesh axis runs over, the one named last changes fastest.
Arguments:
- anomalies: bfloat16 [8, 136, 128, 2048], P('mode', None, 'space'), may hold values from -6 to 6
- vector: float32 [136, 128, 2048], P(None, 'space'), may hold values from -6 to 6
- modes: float32 [16, 136], P('mode'), may hold values from -0.5 to 0.5
- order: int32 [8], replicated, may hold values from 0 to 7, each once
- weights: float32 [8], replicated, may hold values from 0.3 to 3
- diffusivity: float32 [128, 2048], P('space'), may hold values from 0.04 to 0.24
Outputs:
- increment: float32 [136, 128, 2048], P('mode', 'space')
Inputs may be any that keep to these rules, and one draw needn't show every extreme that they name: `order`: each member appears once.
All inputs are finite; a program needn't handle non-finite values.
Results may differ from a plain program's by a relative error of at most 0.0003.
Values may be sent and summed in bfloat16 or wider, within the bound.
A program may use at most 128 MiB of HBM per device.

v0:
```python
import jax
import jax.numpy as jnp
from jax import lax
from jax.sharding import PartitionSpec as P

DIFF = 4


def extended(cells, sides, width):
    for axis, dim in sides:
        count = lax.axis_size(axis)
        ends = count - 1
        head = lax.slice_in_dim(cells, 0, width, axis=dim)
        tail = lax.slice_in_dim(cells, cells.shape[dim] - width, cells.shape[dim], axis=dim)
        cells = jnp.concatenate(
            [
                lax.ppermute(tail, axis, [(i, (i + 1) % count) for i in range(ends)]),
                cells,
                lax.ppermute(head, axis, [((i + 1) % count, i) for i in range(ends)]),
            ],
            axis=dim,
        )
    return cells


def broadcast(block, axis, owner):
    block = jnp.where(lax.axis_index(axis) == owner, block, jnp.zeros_like(block))
    return lax.psum(block, axis)


def sweep(padded, coeff):
    centre = padded[:, 1:-1]
    here = coeff[1:-1]
    total = centre + 0.5 * (here + coeff[2:]) * (padded[:, 2:] - centre)
    total = total + 0.5 * (here + coeff[:-2]) * (padded[:, :-2] - centre)
    east = jnp.roll(here, -1, axis=1)
    west = jnp.roll(here, 1, axis=1)
    total = total + 0.5 * (here + east) * (jnp.roll(centre, -1, axis=2) - centre)
    total = total + 0.5 * (here + west) * (jnp.roll(centre, 1, axis=2) - centre)
    return total


def diffuse(fields, coeff_ext):
    rows = fields.shape[1]
    near = coeff_ext[DIFF - 1 : DIFF + rows + 1]
    for sweep_index in range(DIFF):
        padded = extended(fields, (("space", 1),), 1)
        fields = sweep(padded, near)
    return fields


def contribution(member_field, vector, modes, weight, coeff_ext):
    xf = member_field.astype(jnp.float32)
    product = xf * vector
    projected = jnp.einsum("kl,lan->kan", modes, product, precision=lax.Precision.HIGHEST)
    fields = diffuse(projected, coeff_ext)
    back = jnp.einsum("kl,kan->lan", modes, fields, precision=lax.Precision.HIGHEST)
    return weight * xf * back


def body(anomalies, vector, modes, order, weights, diffusivity):
    coeff_ext = extended(diffusivity, (("space", 0),), DIFF)
    slots = anomalies.shape[0]
    empty = jnp.zeros(vector.shape, jnp.float32)

    def step(index, total):
        member = order[index]
        holder = member // slots
        slot = member % slots
        mine = lax.dynamic_index_in_dim(anomalies, slot, 0, keepdims=False)
        member_field = broadcast(mine, "mode", holder)
        return total + contribution(member_field, vector, modes, weights[index], coeff_ext)

    partial_sum = lax.fori_loop(0, order.shape[0], step, empty)
    return lax.psum_scatter(partial_sum, "mode", scatter_dimension=0, tiled=True)


def solution(mesh):
    return jax.shard_map(
        body,
        mesh=mesh,
        in_specs=(
            P("mode", None, "space", None),
            P(None, "space", None),
            P("mode", None),
            P(),
            P(),
            P("space", None),
        ),
        out_specs=P("mode", "space", None),
        check_vma=False,
    )
```

profile of v0, /device:TPU:30, one launch (start us, length us, event | category | flops | bytes accessed | tf_op | source)
XLA Modules:
  0.0 1378.2 jit_solution(713803589068910227)
XLA Ops:
  10.1 7.3 collective-permute-start.9
  19.1 7.0 copy.11
  27.6 1212.3 %while.16 = (s32[]{:T(128)}, f32[136,4,2048]{2,0,1:T(8,128)}, f32[8]{0:T(128)S(1)}, s32[8]{0:T(128)S(1)}, bf16[1,136,4,2048]{3,1,2,0:T(8,128)(2,1)S(1)}, /*index...) while((s32[]{:T(128)}, f32[136,4,2048]{2,0,1:T(8,128)}, ...), condition=%wide.region_2.3_spmd.clone, body=%wide.region_0.2_spmd.clone.sunk | while | flops 64585736 | bytes 84019992 | solution.py:74
  31.2 88.4 %all-reduce.6.cloned.1.call-done = bf16[136,4,2048]{2,0,1:T(8,128)(2,1)} async-done(((bf16[136,4,2048]{2,0,1:T(8,128)(2,1)}), bf16[136,4,2048]{2,0,1:T(8,128)(2,1)}) %all-reduce.6.cloned.1.call-update) | async-done | bytes 2228240 | tf_op jit(solution)/shard_map/while/body/eval_jaxpr/psum | solution.py:28
  155.7 5.8 collective-permute-done.5
  167.8 5.8 collective-permute-done.7
  173.6 6.6 fusion.116
  185.8 85.2 %all-reduce.6.cloned.1.call-done = bf16[136,4,2048]{2,0,1:T(8,128)(2,1)} async-done(((bf16[136,4,2048]{2,0,1:T(8,128)(2,1)}), bf16[136,4,2048]{2,0,1:T(8,128)(2,1)}) %all-reduce.6.cloned.1.call-update) | async-done | bytes 2228240 | tf_op jit(solution)/shard_map/while/body/eval_jaxpr/psum | solution.py:28
  282.9 5.8 collective-permute-done.1
  325.0 6.6 fusion.116
  337.1 85.0 %all-reduce.6.cloned.1.call-done = bf16[136,4,2048]{2,0,1:T(8,128)(2,1)} async-done(((bf16[136,4,2048]{2,0,1:T(8,128)(2,1)}), bf16[136,4,2048]{2,0,1:T(8,128)(2,1)}) %all-reduce.6.cloned.1.call-update) | async-done | bytes 2228240 | tf_op jit(solution)/shard_map/while/body/eval_jaxpr/psum | solution.py:28
  476.1 6.6 fusion.116
  488.3 84.6 %all-reduce.6.cloned.1.call-done = bf16[136,4,2048]{2,0,1:T(8,128)(2,1)} async-done(((bf16[136,4,2048]{2,0,1:T(8,128)(2,1)}), bf16[136,4,2048]{2,0,1:T(8,128)(2,1)}) %all-reduce.6.cloned.1.call-update) | async-done | bytes 2228240 | tf_op jit(solution)/shard_map/while/body/eval_jaxpr/psum | solution.py:28
  626.9 6.6 fusion.116
  639.0 84.9 %all-reduce.6.cloned.1.call-done = bf16[136,4,2048]{2,0,1:T(8,128)(2,1)} async-done(((bf16[136,4,2048]{2,0,1:T(8,128)(2,1)}), bf16[136,4,2048]{2,0,1:T(8,128)(2,1)}) %all-reduce.6.cloned.1.call-update) | async-done | bytes 2228240 | tf_op jit(solution)/shard_map/while/body/eval_jaxpr/psum | solution.py:28
  777.9 6.6 fusion.116
  790.0 85.0 %all-reduce.6.cloned.1.call-done = bf16[136,4,2048]{2,0,1:T(8,128)(2,1)} async-done(((bf16[136,4,2048]{2,0,1:T(8,128)(2,1)}), bf16[136,4,2048]{2,0,1:T(8,128)(2,1)}) %all-reduce.6.cloned.1.call-update) | async-done | bytes 2228240 | tf_op jit(solution)/shard_map/while/body/eval_jaxpr/psum | solution.py:28
  929.1 6.6 fusion.116
  941.2 84.9 %all-reduce.6.cloned.1.call-done = bf16[136,4,2048]{2,0,1:T(8,128)(2,1)} async-done(((bf16[136,4,2048]{2,0,1:T(8,128)(2,1)}), bf16[136,4,2048]{2,0,1:T(8,128)(2,1)}) %all-reduce.6.cloned.1.call-update) | async-done | bytes 2228240 | tf_op jit(solution)/shard_map/while/body/eval_jaxpr/psum | solution.py:28
  1080.1 6.6 fusion.116
  1092.3 84.9 %all-reduce.6.cloned.1.call-done = bf16[136,4,2048]{2,0,1:T(8,128)(2,1)} async-done(((bf16[136,4,2048]{2,0,1:T(8,128)(2,1)}), bf16[136,4,2048]{2,0,1:T(8,128)(2,1)}) %all-reduce.6.cloned.1.call-update) | async-done | bytes 2228240 | tf_op jit(solution)/shard_map/while/body/eval_jaxpr/psum | solution.py:28
  1231.2 6.6 fusion.116
  1239.9 7.2 copy.12
  1249.0 119.8 %all-reduce.4.cloned.1.call-done = f32[136,4,2048]{2,1,0:T(4,128)} async-done(((f32[136,4,2048]{2,1,0:T(4,128)}), f32[136,4,2048]{2,1,0:T(4,128)}) %all-reduce.4.cloned.1.call-update) | async-done | bytes 4456464
  (381 shorter events, 461.7 us)
Async XLA Ops:
  7.4 20.0 %collective-permute-start.8 = (f32[4,2048]{1,0:T(4,128)}, f32[4,2048]{1,0:T(4,128)S(1)}, u32[]{:S(2)}, u32[]{:S(2)}) collective-permute-start(f32[4,2048]{1,0:T(4,128)} %param.13), channel_id=1, source_target_pairs={{1,0},{2,1},{3,2},{4,3},{5,4},{6,5},{7,6},{8,7},{9,8},{10,9},{11,1... | collective-permute-start | bytes 98312 | tf_op jit(solution)/shard_map/ppermute | solution.py:19
  10.1 17.3 %collective-permute-start.9 = (f32[4,2048]{1,0:T(4,128)}, f32[4,2048]{1,0:T(4,128)S(1)}, u32[]{:S(2)}, u32[]{:S(2)}) collective-permute-start(f32[4,2048]{1,0:T(4,128)} %param.13), channel_id=1, source_target_pairs={{0,1},{1,2},{2,3},{3,4},{4,5},{5,6},{6,7},{7,8},{8,9},{9,10},{10,1... | collective-permute-start | bytes 98312 | tf_op jit(solution)/shard_map/ppermute | solution.py:17
  27.8 91.9 %all-reduce.6.cloned.1.call-start = ((), (), s32[]{:S(2)}) async-start(), calls=%async_computation.1 | async-start | bytes 4456448 | tf_op jit(solution)/shard_map/while/body/eval_jaxpr/psum | solution.py:28
  127.5 9.9 collective-permute-start.1
  139.6 9.9 collective-permute-start.3
  151.7 9.9 collective-permute-start.5
  163.8 9.9 collective-permute-start.7
  182.3 88.7 %all-reduce.6.cloned.1.call-start = ((), (), s32[]{:S(2)}) async-start(), calls=%async_computation.1 | async-start | bytes 4456448 | tf_op jit(solution)/shard_map/while/body/eval_jaxpr/psum | solution.py:28
  278.8 9.9 collective-permute-start.1
  290.9 9.9 collective-permute-start.3
  303.0 9.9 collective-permute-start.5
  315.1 9.9 collective-permute-start.7
  333.7 88.5 %all-reduce.6.cloned.1.call-start = ((), (), s32[]{:S(2)}) async-start(), calls=%async_computation.1 | async-start | bytes 4456448 | tf_op jit(solution)/shard_map/while/body/eval_jaxpr/psum | solution.py:28
  442.1 9.9 collective-permute-start.3
  454.2 9.9 collective-permute-start.5
  466.3 9.9 collective-permute-start.7
  484.8 88.0 %all-reduce.6.cloned.1.call-start = ((), (), s32[]{:S(2)}) async-start(), calls=%async_computation.1 | async-start | bytes 4456448 | tf_op jit(solution)/shard_map/while/body/eval_jaxpr/psum | solution.py:28
  580.8 9.9 collective-permute-start.1
  592.8 9.9 collective-permute-start.3
  635.6 88.3 %all-reduce.6.cloned.1.call-start = ((), (), s32[]{:S(2)}) async-start(), calls=%async_computation.1 | async-start | bytes 4456448 | tf_op jit(solution)/shard_map/while/body/eval_jaxpr/psum | solution.py:28
  786.6 88.5 %all-reduce.6.cloned.1.call-start = ((), (), s32[]{:S(2)}) async-start(), calls=%async_computation.1 | async-start | bytes 4456448 | tf_op jit(solution)/shard_map/while/body/eval_jaxpr/psum | solution.py:28
  937.8 88.4 %all-reduce.6.cloned.1.call-start = ((), (), s32[]{:S(2)}) async-start(), calls=%async_computation.1 | async-start | bytes 4456448 | tf_op jit(solution)/shard_map/while/body/eval_jaxpr/psum | solution.py:28
  1088.8 88.4 %all-reduce.6.cloned.1.call-start = ((), (), s32[]{:S(2)}) async-start(), calls=%async_computation.1 | async-start | bytes 4456448 | tf_op jit(solution)/shard_map/while/body/eval_jaxpr/psum | solution.py:28
  1239.9 128.9 %all-reduce.4.cloned.1.call-start = ((), (), s32[]{:S(2)}) async-start(), calls=%async_computation | async-start | bytes 8912896
  (81 other events, 1270.8 us)
Sparse Core Ops, SparseCore 0:
  31.3 88.3 all-reduce.5
  185.8 85.1 all-reduce.5
  337.2 84.9 all-reduce.5
  488.0 84.8 all-reduce.5
  638.8 85.0 all-reduce.5
  789.8 85.2 all-reduce.5
  941.3 84.8 all-reduce.5
  1092.3 84.8 all-reduce.5
Sparse Core Ops, SparseCore 1:
  1247.2 121.6 all-reduce.3
where the time goes:
time: 1380 us
  waiting for transfers between devices  990 us (72%)
  starting transfers between devices  197 us (14%)
  matrix products  99 us (7%)
  local copies, waits for them, and re-layouts  52.8 us (4%)
  other arithmetic  17.4 us (1%)
  between operations  15.6 us (1%)
    psum x8, waiting for transfers between devices, broadcast(): return lax.psum(block, axis)  683 us
    ppermute x33, waiting for transfers between devices, extended(): lax.ppermute(head, axis, [((i + 1) % count, i) for i in range(ends)])  187 us
    ppermute x33, starting transfers between devices, extended(): lax.ppermute(head, axis, [((i + 1) % count, i) for i in range(ends)])  128 us
    unnamed x2, waiting for transfers between devices  120 us
    ppermute x33, starting transfers between devices, extended(): lax.ppermute(tail, axis, [(i, (i + 1) % count) for i in range(ends)])  68.8 us
    dot_general x8, matrix products, contribution(): jnp.einsum('kl,kan->lan', modes, fields, precision=lax.Precision.HIGHEST)  52.9 us
    dot_general x8, matrix products, contribution(): jnp.einsum('kl,lan->kan', modes, product, precision=lax.Precision.HIGHEST)  46.2 us
  transfers between devices with their start and end apart: 75, of which 41 were waited for; matrix products, arithmetic and copies ran while one was open for 1% of the time, Pallas kernels for 0%

commit v1 on v0

v1 whole, which is shorter than its diff:
```python
import jax
import jax.numpy as jnp
from jax import lax
from jax.sharding import PartitionSpec as P

DIFF = 4


def extended(cells, axis, dim, width):
    count = lax.axis_size(axis)
    ends = count - 1
    head = lax.slice_in_dim(cells, 0, width, axis=dim)
    tail = lax.slice_in_dim(cells, cells.shape[dim] - width, cells.shape[dim], axis=dim)
    return jnp.concatenate(
        [
            lax.ppermute(tail, axis, [(i, (i + 1) % count) for i in range(ends)]),
            cells,
            lax.ppermute(head, axis, [((i + 1) % count, i) for i in range(ends)]),
        ],
        axis=dim,
    )


def sweep(padded, coeff):
    centre = padded[:, 1:-1]
    here = coeff[1:-1]
    total = centre + 0.5 * (here + coeff[2:]) * (padded[:, 2:] - centre)
    total = total + 0.5 * (here + coeff[:-2]) * (padded[:, :-2] - centre)
    east = jnp.roll(here, -1, axis=1)
    west = jnp.roll(here, 1, axis=1)
    total = total + 0.5 * (here + east) * (jnp.roll(centre, -1, axis=2) - centre)
    total = total + 0.5 * (here + west) * (jnp.roll(centre, 1, axis=2) - centre)
    return total


def body(anomalies, vector, modes, order, weights, diffusivity):
    rows = diffusivity.shape[0]
    me = lax.axis_index("mode")
    place = lax.axis_index("space")
    last = lax.axis_size("space") - 1
    modes = lax.all_gather(modes, "mode", axis=0, tiled=True)
    weight = jnp.sum(jnp.where(order == me, weights, 0.0))
    coeff = extended(diffusivity, "space", 0, DIFF)
    xf = anomalies[0].astype(jnp.float32)
    projected = jnp.einsum("kl,lan->kan", modes, xf * vector, precision=lax.Precision.HIGHEST)
    fields = extended(projected, "space", 1, DIFF)
    index = jnp.arange(rows + 2 * DIFF)
    inside = ((index >= DIFF) | (place > 0)) & ((index < rows + DIFF) | (place < last))
    for done in range(1, DIFF + 1):
        stop = rows + 2 * DIFF - done
        fields = sweep(fields, coeff[done - 1 : stop + 1])
        fields = jnp.where(inside[done:stop][None, :, None], fields, 0.0)
    back = jnp.einsum("kl,kan->lan", modes, fields, precision=lax.Precision.HIGHEST)
    return lax.psum_scatter(weight * xf * back, "mode", scatter_dimension=0, tiled=True)


def solution(mesh):
    return jax.shard_map(
        body,
        mesh=mesh,
        in_specs=(
            P("mode", None, "space", None),
            P(None, "space", None),
            P("mode", None),
            P(),
            P(),
            P("space", None),
        ),
        out_specs=P("mode", "space", None),
        check_vma=False,
    )
```

time: 1380 us -> 213 us (0.15)
  waiting for transfers between devices: 990 us -> 135 us
  starting transfers between devices: 197 us -> 14.7 us
  matrix products: 99 us -> 15.6 us
  local copies, waits for them, and re-layouts: 52.8 us -> 11.8 us
  blocking collectives: 0 us -> 18.3 us
  other arithmetic: 17.4 us -> 3.09 us
    psum x8 -> x0, waiting for transfers between devices: 683 us -> none  [broadcast(): return lax.psum(block, axis)]
    ppermute x33 -> x2, waiting for transfers between devices: 187 us -> 8.34 us  [extended(): lax.ppermute(head, axis, [((i + 1) % count, i) for i in range(ends)])]
    ppermute x33 -> x2, starting transfers between devices: 128 us -> 4.55 us  [extended(): lax.ppermute(head, axis, [((i + 1) % count, i) for i in range(ends)])]
    dot_general x16 -> x2, matrix products: 99 us -> 15.6 us  [the longest x1 8.44 us: body(): jnp.einsum('kl,lan->kan', modes, xf * vector, precision=lax.Precision.HIG...]
    ppermute x33 -> x2, starting transfers between devices: 68.8 us -> 10.1 us  [extended(): lax.ppermute(tail, axis, [(i, (i + 1) % count) for i in range(ends)])]
    while x49 -> x0, local copies, waits for them, and re-layouts: 23.8 us -> none
    all_gather x0 -> x1, blocking collectives: none -> 18.3 us  [body(): modes = lax.all_gather(modes, 'mode', axis=0, tiled=True)]
  transfers between devices with their start and end apart: 75 -> 5, of which waited for: 41 -> 3; matrix products, arithmetic and copies ran while one was open for 1% -> 5% of each run, Pallas kernels for 0% -> 0%
where the time goes in v1:
time: 213 us
  waiting for transfers between devices  135 us (63%)
  blocking collectives  18.3 us (9%)
  matrix products  15.6 us (7%)
  starting transfers between devices  14.7 us (7%)
  between operations  14.2 us (7%)
  local copies, waits for them, and re-layouts  11.8 us (6%)
  other arithmetic  3.09 us (1%)
    unnamed x2, waiting for transfers between devices  119 us
    all_gather x1, blocking collectives, body(): modes = lax.all_gather(modes, 'mode', axis=0, tiled=True)  18.3 us
    ppermute x2, starting transfers between devices, extended(): lax.ppermute(tail, axis, [(i, (i + 1) % count) for i in range(ends)])  10.1 us
    dot_general x1, matrix products, body(): jnp.einsum('kl,lan->kan', modes, xf * vector, precision=lax.Precision.HIG...  8.44 us
    ppermute x2, waiting for transfers between devices, extended(): lax.ppermute(head, axis, [((i + 1) % count, i) for i in range(ends)])  8.34 us
    ppermute x2, waiting for transfers between devices, extended(): lax.ppermute(tail, axis, [(i, (i + 1) % count) for i in range(ends)])  7.62 us
    dot_general x1, matrix products, body(): jnp.einsum('kl,kan->lan', modes, fields, precision=lax.Precision.HIGHEST)  7.12 us
    mul x1, local copies, waits for them, and re-layouts, body(): weight * xf * back  4.95 us
  transfers between devices with their start and end apart: 5, of which 3 were waited for; matrix products, arithmetic and copies ran while one was open for 5% of the time, Pallas kernels for 0%

profile of v1, /device:TPU:30, one launch (start us, length us, event | category | flops | bytes accessed | tf_op | source)
XLA Modules:
  0.0 212.6 jit_solution(10777589421947758380)
XLA Ops:
  6.5 3.4 %collective-permute-start.2 = (f32[4,2048]{1,0:T(4,128)}, f32[4,2048]{1,0:T(4,128)S(1)}, u32[]{:S(2)}, u32[]{:S(2)}) collective-permute-start(f32[4,2048]{1,0:T(4,128)} %param.11), channel_id=1, source_target_pairs={{0,1},{1,2},{2,3},{3,4},{4,5},{5,6},{6,7},{7,8},{8,9},{9,10},{10,1... | collective-permute-start | bytes 98312 | tf_op jit(solution)/shard_map/ppermute | solution.py:16
  9.9 2.4 %collective-permute-start.3 = (f32[4,2048]{1,0:T(4,128)}, f32[4,2048]{1,0:T(4,128)S(1)}, u32[]{:S(2)}, u32[]{:S(2)}) collective-permute-start(f32[4,2048]{1,0:T(4,128)} %param.11), channel_id=1, source_target_pairs={{1,0},{2,1},{3,2},{4,3},{5,4},{6,5},{7,6},{8,7},{9,8},{10,9},{11,1... | collective-permute-start | bytes 98312 | tf_op jit(solution)/shard_map/ppermute | solution.py:18
  12.4 18.3 %all-gather = f32[8,2,136]{2,1,0:T(2,128)S(1)} all-gather(f32[1,2,136]{2,1,0:T(2,128)} %bitcast.15), channel_id=1, replica_groups=mesh['mode'=8,'space'=32] {'mode'}, dimensions={0}, use_global_device_ids=true | all-gather | bytes 9792 | tf_op jit(solution)/shard_map/all_gather | solution.py:41
  30.8 8.4 %fusion.3 = f32[16,4,2048]{2,0,1:T(8,128)S(1)} fusion(f32[16,136,1]{1,0,2:T(8,128)S(1)} %reshape.25, f32[136,4,2048]{2,1,0:T(4,128)} %param.7, bf16[1,136,4,2048]{3,2,1,0:T(4,128)(2,1)} %param.6), kind=kOutput, calls=%fused_computation.5 | convolution fusion | flops 216137728 | bytes 7217664 | tf_op jit(solution)/shard_map/kl,lan->kan/dot_general | solution.py:45
  39.2 6.7 %collective-permute-start = (f32[16,4,2048]{2,0,1:T(8,128)S(1)}, f32[16,4,2048]{2,0,1:T(8,128)S(1)}, u32[]{:S(2)}, u32[]{:S(2)}) collective-permute-start(f32[16,4,2048]{2,0,1:T(8,128)S(1)} %fusion.3), channel_id=1, source_target_pairs={{0,1},{1,2},{2,3},{3,4},{4,5},{5,6},{6,7},{7,8},{8,9},{9,10},{10,1... | collective-permute-start | bytes 1572872 | tf_op jit(solution)/shard_map/ppermute | solution.py:16
  46.0 2.1 collective-permute-start.1
  48.2 0.6 fusion.87
  49.9 0.1 fusion.62
  50.0 7.6 %collective-permute-done = f32[16,4,2048]{2,0,1:T(8,128)S(1)} collective-permute-done((f32[16,4,2048]{2,0,1:T(8,128)S(1)}, f32[16,4,2048]{2,0,1:T(8,128)S(1)}, u32[]{:S(2)}, u32[]{:S(2)}) %collective-permute-start) | collective-permute-done | bytes 524320 | tf_op jit(solution)/shard_map/ppermute | solution.py:16
  57.6 8.3 %collective-permute-done.1 = f32[16,4,2048]{2,0,1:T(8,128)S(1)} collective-permute-done((f32[16,4,2048]{2,0,1:T(8,128)S(1)}, f32[16,4,2048]{2,0,1:T(8,128)S(1)}, u32[]{:S(2)}, u32[]{:S(2)}) %collective-permute-start.1) | collective-permute-done | bytes 524320 | tf_op jit(solution)/shard_map/ppermute | solution.py:18
  66.0 0.5 fusion.90
  66.5 0.8 fusion.10
  67.3 0.4 fusion.92
  67.8 0.6 fusion.23
  68.4 0.3 fusion.94
  68.8 0.5 fusion.32
  69.3 0.2 fusion.96
  69.6 1.3 copy-done
  70.9 7.1 %fusion = f32[136,4,2048]{2,0,1:T(8,128)S(1)} fusion(f32[16,136,1]{1,0,2:T(8,128)S(1)} %reshape.25, f32[]{:T(128)} %fusion.87, bf16[1,136,4,2048]{3,2,1,0:T(4,128)(2,1)S(1)} %copy-done, f32[16,6,2048]{2,0,1:T(8,128)S(1)} %fusion.32, f32[16,4,1]{2,0,1:T(8,128)S(1)} %get-tuple-element.16, f32[16,4,2047]{2,0,1:T(8,128)S(1)} %get-tuple-element.18, ...), kind=kOutput, calls=%fused_computation.2 | convolution fusion | flops 219217920 | bytes 9519620 | tf_op jit(solution)/shard_map/kl,kan->lan/dot_general | solution.py:53
  78.0 5.0 %copy.12 = f32[136,4,2048]{2,1,0:T(4,128)} copy(f32[136,4,2048]{2,0,1:T(8,128)S(1)} %fusion) | data formatting | bytes 8912896 | tf_op jit(solution)/shard_map/mul | solution.py:54
  83.0 0.6 copy-done.4
  83.7 0.6 dynamic-slice
  84.9 119.0 %all-reduce.3.cloned.1.call-done = f32[136,4,2048]{2,1,0:T(4,128)} async-done(((f32[136,4,2048]{2,1,0:T(4,128)}), f32[136,4,2048]{2,1,0:T(4,128)}) %all-reduce.3.cloned.1.call-update) | async-done | bytes 4456464
  203.9 1.9 constant_dynamic-slice_fusion
  (32 shorter events, 1.5 us)
Async XLA Ops:
  6.5 197.3 %all-reduce.3.cloned.1.call-start = ((), (), s32[]{:S(2)}) async-start(), calls=%async_computation | async-start | bytes 8912896
  6.5 42.6 %collective-permute-start.2 = (f32[4,2048]{1,0:T(4,128)}, f32[4,2048]{1,0:T(4,128)S(1)}, u32[]{:S(2)}, u32[]{:S(2)}) collective-permute-start(f32[4,2048]{1,0:T(4,128)} %param.11), channel_id=1, source_target_pairs={{0,1},{1,2},{2,3},{3,4},{4,5},{5,6},{6,7},{7,8},{8,9},{9,10},{10,1... | collective-permute-start | bytes 98312 | tf_op jit(solution)/shard_map/ppermute | solution.py:16
  9.9 39.2 %collective-permute-start.3 = (f32[4,2048]{1,0:T(4,128)}, f32[4,2048]{1,0:T(4,128)S(1)}, u32[]{:S(2)}, u32[]{:S(2)}) collective-permute-start(f32[4,2048]{1,0:T(4,128)} %param.11), channel_id=1, source_target_pairs={{1,0},{2,1},{3,2},{4,3},{5,4},{6,5},{7,6},{8,7},{9,8},{10,9},{11,1... | collective-permute-start | bytes 98312 | tf_op jit(solution)/shard_map/ppermute | solution.py:18
  30.8 17.3 %copy-start.1 = (f32[4,2048]{1,0:T(4,128)S(1)}, f32[4,2048]{1,0:T(4,128)}, u32[]{:S(2)}) copy-start(f32[4,2048]{1,0:T(4,128)} %param.11) | copy-start | bytes 98308
  30.8 17.5 %copy-start.2 = (f32[8]{0:T(128)S(1)}, f32[8]{0:T(128)}, u32[]{:S(2)}) copy-start(f32[8]{0:T(128)} %param.10) | copy-start | bytes 100
  30.8 17.5 %copy-start.3 = (s32[8]{0:T(128)S(1)}, s32[8]{0:T(128)}, u32[]{:S(2)}) copy-start(s32[8]{0:T(128)} %param.9) | copy-start | bytes 100
  39.2 18.4 %collective-permute-start = (f32[16,4,2048]{2,0,1:T(8,128)S(1)}, f32[16,4,2048]{2,0,1:T(8,128)S(1)}, u32[]{:S(2)}, u32[]{:S(2)}) collective-permute-start(f32[16,4,2048]{2,0,1:T(8,128)S(1)} %fusion.3), channel_id=1, source_target_pairs={{0,1},{1,2},{2,3},{3,4},{4,5},{5,6},{6,7},{7,8},{8,9},{9,10},{10,1... | collective-permute-start | bytes 1572872 | tf_op jit(solution)/shard_map/ppermute | solution.py:16
  46.0 20.0 %collective-permute-start.1 = (f32[16,4,2048]{2,0,1:T(8,128)S(1)}, f32[16,4,2048]{2,0,1:T(8,128)S(1)}, u32[]{:S(2)}, u32[]{:S(2)}) collective-permute-start(f32[16,4,2048]{2,0,1:T(8,128)S(1)} %fusion.3), channel_id=1, source_target_pairs={{1,0},{2,1},{3,2},{4,3},{5,4},{6,5},{7,6},{8,7},{9,8},{10,9},{11,1... | collective-permute-start | bytes 1572872 | tf_op jit(solution)/shard_map/ppermute | solution.py:18
  69.3 1.6 copy-start
  83.0 0.7 copy-start.4
Sparse Core Ops, SparseCore 0:
  83.1 120.6 all-reduce.2

commit v2 on v1

v2 whole, which is shorter than its diff:
```python
import jax
import jax.numpy as jnp
from jax import lax
from jax.experimental import pallas as pl
from jax.experimental.pallas import tpu as pltpu
from jax.sharding import PartitionSpec as P

LEV, NLON, DIFF, MODES, ROWS = 136, 2048, 4, 16, 4
GROUPS = 8
GLEV = LEV // GROUPS
TILES = NLON // 128
CHUNKS = 4
SUB = TILES * ROWS // CHUNKS
WIDE = NLON // CHUNKS
PADDED = NLON + 256
EXT = ROWS + 2 * DIFF
HALF = (GLEV + 1) // 2
MSGS = CHUNKS + 1
TINY = 1e-33
F32, BF16, I16 = jnp.float32, jnp.bfloat16, jnp.int16


def split(a):
    hi = a.astype(BF16)
    return hi, (a - hi.astype(F32)).astype(BF16)


def pack(a, top):
    return jnp.round(a * (32767.0 / top)).astype(I16)


def kernel(x_hbm, v_hbm, modes_hbm, order_ref, weights_ref, diff_hbm, out_ref,
           xs, vs, mine, nu, mall, nuext, phi, plo, spread, pick, fwd, bwd, field, coef, loc, lcat,
           hq, hsc, hqr, hscr, sib, sibr, own, zq1, zs1, zq1r, zs1r, zqa, zqb, zs2, zqar, zqbr, zs2r,
           lsem, m_s, m_r, d_s, d_r, hq_s, hq_r, hs_s, hs_r, sb_s, sb_r,
           z1_s, z1_r, t1_s, t1_r, z2_s, z2_r, t2_s, t2_r):
    me = lax.axis_index("mode")
    place = lax.axis_index("space")
    ring, core = me // 2, me % 2
    has_prev = place > 0
    has_next = place < lax.axis_size("space") - 1
    right = {"mode": ((ring + 1) % 4) * 2 + core}
    left = {"mode": ((ring + 3) % 4) * 2 + core}
    partner = {"mode": ring * 2 + 1 - core}
    before, after = {"space": place - 1}, {"space": place + 1}

    def remote(src, dst, ss, rs, dev):
        return pltpu.make_async_remote_copy(
            src_ref=src, dst_ref=dst, send_sem=ss, recv_sem=rs, device_id=dev,
            device_id_type=pl.DeviceIdType.MESH)

    def chunk_rows(n):
        return pl.ds(pl.multiple_of(n * SUB, SUB), SUB)

    get_modes = pltpu.make_async_copy(modes_hbm, mine, lsem.at[0])
    get_nu = pltpu.make_async_copy(diff_hbm, nu, lsem.at[1])

    def get_x(n):
        return pltpu.make_async_copy(x_hbm.at[:, chunk_rows(n)], xs.at[:, chunk_rows(n)], lsem.at[2 + n])

    def get_v(n):
        return pltpu.make_async_copy(v_hbm.at[:, chunk_rows(n)], vs.at[:, chunk_rows(n)], lsem.at[2 + CHUNKS + n])

    get_modes.start()
    get_nu.start()
    for n in range(CHUNKS):
        get_x(n).start()
        get_v(n).start()

    barrier = pltpu.get_barrier_semaphore()

    def greet(dev):
        pl.semaphore_signal(barrier, inc=1, device_id=dev, device_id_type=pl.DeviceIdType.MESH)

    for j in range(1, GROUPS):
        greet({"mode": (me + j) % GROUPS})
    pl.when(has_prev)(lambda: greet(before))
    pl.when(has_next)(lambda: greet(after))

    lane_level = lax.broadcasted_iota(jnp.int32, (256, LEV * 8), 1) >> 3
    spread[...] = jnp.where(lane_level == lax.broadcasted_iota(jnp.int32, (256, LEV * 8), 0), 1.0, 0.0).astype(BF16)
    for i in range(GROUPS):
        c = 1 - core if i < 4 else core
        group = ((ring + i) % 4) * 2 + c
        level = group * GLEV + (lax.broadcasted_iota(jnp.int32, (LEV, 256), 0) >> 3)
        pick[i // 4, (i % 4) * LEV : (i % 4 + 1) * LEV, :] = jnp.where(
            lax.broadcasted_iota(jnp.int32, (LEV, 256), 1) == level, 1.0, 0.0).astype(BF16)

    get_modes.wait()
    which = lax.broadcasted_iota(jnp.int32, (MODES, LEV), 0) - 2 * me
    block = jnp.where(which == 0, mine[0:1, :], jnp.where(which == 1, mine[1:2, :], 0.0))
    mall[0] = jnp.concatenate([block, jnp.zeros((MODES, 256 - LEV), F32)], axis=1)
    get_nu.wait()

    def products(n):
        get_x(n).wait()
        get_v(n).wait()

        def part(b, carry):
            lev = pl.ds(b * 8, 8)
            p = xs[lev, chunk_rows(n), :].astype(F32) * vs[lev, chunk_rows(n), :]
            for h in range(2):
                hi, lo = split(p[:, 8 * h : 8 * h + 8, :].reshape(64, 128))
                at = pl.ds(pl.multiple_of(b * 64, 64), 64)
                phi[n, at, 128 * h : 128 * h + 128] = hi
                plo[n, at, 128 * h : 128 * h + 128] = lo
            return carry

        lax.fori_loop(0, LEV // 8, part, 0)

    products(0)
    pl.semaphore_wait(barrier, GROUPS - 1 + has_prev.astype(jnp.int32) + has_next.astype(jnp.int32))

    def send_modes(j):
        return remote(mall.at[0], mall.at[j], m_s.at[j], m_r.at[j], {"mode": (me + j) % GROUPS})

    for j in range(1, GROUPS):
        send_modes(j).start()
    nu_up = remote(nu, nuext.at[0], d_s.at[0], d_r.at[0], after)
    nu_down = remote(nu, nuext.at[1], d_s.at[1], d_r.at[1], before)
    pl.when(has_next)(lambda: nu_up.start())
    pl.when(has_prev)(lambda: nu_down.start())

    for n in range(1, CHUNKS):
        products(n)

    for j in range(1, GROUPS):
        send_modes(j).wait_recv()
    modes = mall[0]
    for j in range(1, GROUPS):
        modes = modes + mall[j]
    modes_hi, modes_lo = split(modes)

    both = jnp.dot(jnp.concatenate([modes_hi, modes_lo], axis=0), spread[...], preferred_element_type=F32)
    sub = lax.broadcasted_iota(jnp.int32, (MODES, LEV * 8), 1) & 7
    for half in range(2):
        rows = both[half * MODES : (half + 1) * MODES]
        for q in range(8):
            fwd[half * 128 + q * MODES : half * 128 + (q + 1) * MODES, :] = jnp.where(sub == q, rows, 0.0).astype(BF16)

    def project(n):
        main = jnp.dot(fwd[...], phi[n], preferred_element_type=F32)
        rest = jnp.dot(fwd[0:128, :], plo[n], preferred_element_type=F32)
        total = main[0:128] + main[128:256] + rest
        for par in range(2):
            for r in range(ROWS):
                for h in range(2):
                    at = (1 + 4 * n + 2 * h + par) * 128
                    q = (par * ROWS + r) * MODES
                    field[DIFF + r, :, at : at + 128] = total[q : q + MODES, h * 128 : h * 128 + 128]

    for n in range(CHUNKS):
        project(n)
    field[DIFF : DIFF + ROWS, :, 0:128] = field[DIFF : DIFF + ROWS, :, NLON : NLON + 128]
    field[DIFF : DIFF + ROWS, :, NLON + 128 : PADDED] = field[DIFF : DIFF + ROWS, :, 128:256]

    def halo_lanes(i):
        if isinstance(i, int) and i == 0:
            return pl.ds(0, 256)
        return pl.ds(pl.multiple_of(i * WIDE - WIDE + 256, 128), WIDE)

    def halo(i, way):
        lanes = halo_lanes(i)
        dev = after if way == 0 else before
        return (remote(hq.at[:, :, lanes], hqr.at[way, :, :, lanes], hq_s.at[way, i], hq_r.at[way, i], dev),
                remote(hsc.at[:, lanes], hscr.at[way, :, lanes], hs_s.at[way, i], hs_r.at[way, i], dev))

    def each(copies, what):
        for copy in copies:
            getattr(copy, what)()

    for i in range(MSGS):
        lanes = halo_lanes(i)
        u = field[DIFF : DIFF + ROWS, :, lanes]
        top = jnp.maximum(jnp.max(jnp.max(jnp.abs(u), axis=0), axis=0, keepdims=True), TINY)
        hsc[:, lanes] = top * (1.0 / 32767.0)
        hq[:, :, lanes] = pack(u, top[None])
        pl.when(has_next)(lambda: each(halo(i, 0), "start"))
        pl.when(has_prev)(lambda: each(halo(i, 1), "start"))

    rep_hi = jnp.concatenate([modes_hi] * 8, axis=0)
    rep_lo = jnp.concatenate([modes_lo] * 8, axis=0)
    same = (lax.broadcasted_iota(jnp.int32, (4 * LEV, 128), 0) & 7) == (lax.broadcasted_iota(jnp.int32, (4 * LEV, 128), 1) >> 4)
    last = (((1,), (1,)), ((), ()))
    for part in range(2):
        hi = lax.dot_general(pick[part], rep_hi, last, preferred_element_type=F32)
        lo = lax.dot_general(pick[part], rep_lo, last, preferred_element_type=F32)
        hi = jnp.where(same, hi, 0.0).astype(BF16)
        bwd[part, :, 0:128] = hi
        bwd[part, :, 128:256] = hi
        bwd[part, :, 256:384] = jnp.where(same, lo, 0.0).astype(BF16)

    @pl.when(has_prev)
    def _():
        nu_up.wait_recv()

    @pl.when(has_next)
    def _():
        nu_down.wait_recv()

    @pl.when(jnp.logical_not(has_prev))
    def _():
        nuext[0] = jnp.zeros((ROWS, NLON), F32)
        field[0:DIFF] = jnp.zeros((DIFF, MODES, PADDED), F32)

    @pl.when(jnp.logical_not(has_next))
    def _():
        nuext[1] = jnp.zeros((ROWS, NLON), F32)
        field[DIFF + ROWS : EXT] = jnp.zeros((DIFF, MODES, PADDED), F32)

    def nu_row(a):
        src = nuext[0] if a < DIFF else nu[...] if a < DIFF + ROWS else nuext[1]
        r = a % ROWS
        return jnp.broadcast_to(src[r : r + 1, :], (8, NLON))

    top_mask, low_mask = has_prev.astype(F32), has_next.astype(F32)
    for a in range(1, EXT - 1):
        here = nu_row(a)
        mask = top_mask if a < DIFF else low_mask if a >= DIFF + ROWS else None
        arms = [0.5 * (here + other) for other in (
            nu_row(a - 1), nu_row(a + 1), pltpu.roll(here, NLON - 1, 1), pltpu.roll(here, 1, 1))]
        arms.append(1.0 - (arms[0] + arms[1] + arms[2] + arms[3]))
        for c, arm in enumerate(arms):
            if mask is not None:
                arm = arm * mask
            coef[c, a - 1, :, 128 : NLON + 128] = arm
            coef[c, a - 1, :, 0:128] = arm[:, NLON - 128 : NLON]
            coef[c, a - 1, :, NLON + 128 : PADDED] = arm[:, 0:128]

    weight = jnp.float32(0.0)
    for s in range(GROUPS):
        weight = weight + jnp.where(order_ref[s] == me, weights_ref[s], 0.0)

    def take_halo(i):
        lanes = halo_lanes(i)

        @pl.when(has_prev)
        def _():
            each(halo(i, 0), "wait_recv")
            field[0:DIFF, :, lanes] = hqr[0, :, :, lanes].astype(F32) * hscr[0, :, lanes][None]

        @pl.when(has_next)
        def _():
            each(halo(i, 1), "wait_recv")
            field[DIFF + ROWS : EXT, :, lanes] = hqr[1, :, :, lanes].astype(F32) * hscr[1, :, lanes][None]

    window = WIDE + 256

    def diffuse(n):
        lanes = pl.ds(pl.multiple_of(n * WIDE, 128), window)
        for kh in range(2):
            u = [field[a, kh * 8 : kh * 8 + 8, lanes] for a in range(EXT)]
            for s in range(1, DIFF + 1):
                new = []
                for a in range(s, EXT - s):
                    c, up, down = u[a - s + 1], u[a - s], u[a - s + 2]
                    new.append(
                        coef[4, a - 1, :, lanes] * c
                        + coef[0, a - 1, :, lanes] * up
                        + coef[1, a - 1, :, lanes] * down
                        + coef[2, a - 1, :, lanes] * pltpu.roll(c, window - 1, 1)
                        + coef[3, a - 1, :, lanes] * pltpu.roll(c, 1, 1))
                u = new
            for r in range(ROWS):
                loc[r, kh * 8 : kh * 8 + 8, :] = weight * u[r][:, 128 : 128 + WIDE]
        for par in range(2):
            for r in range(ROWS):
                q = (par * ROWS + r) * MODES
                for h in range(2):
                    t = (2 * h + par) * 128
                    hi, lo = split(loc[r, :, t : t + 128])
                    cols = slice(h * 128, h * 128 + 128)
                    lcat[q : q + MODES, cols] = hi
                    lcat[128 + q : 128 + q + MODES, cols] = lo
                    lcat[256 + q : 256 + q + MODES, cols] = hi

    def backward(n, part, dst):
        back = jnp.dot(bwd[part], lcat[...], preferred_element_type=F32)
        c = core if part else 1 - core
        for i in range(4):
            group = ((ring + i) % 4) * 2 + c
            xg = xs[pl.ds(group * GLEV, GLEV), chunk_rows(n), :].astype(F32)
            for h in range(2):
                b = back[i * LEV : (i + 1) * LEV, h * 128 : h * 128 + 128].reshape(GLEV, 8, 128)
                dst[n, i, :, 8 * h : 8 * h + 8, :] = xg[:, 8 * h : 8 * h + 8, :] * b

    def share(n):
        return remote(sib.at[n], sibr.at[n], sb_s.at[n], sb_r.at[n], partner)

    def first(n, way):
        dev = right if way == 0 else left
        return (remote(zq1.at[n, way], zq1r.at[n, way], z1_s.at[way, n], z1_r.at[way, n], dev),
                remote(zs1.at[n, way], zs1r.at[n, way], t1_s.at[way, n], t1_r.at[way, n], dev))

    def second(n, way):
        dev = right if way == 0 else left
        src, dst = (zqa, zqar) if way == 0 else (zqb, zqbr)
        return (remote(src.at[n], dst.at[n], z2_s.at[way, n], z2_r.at[way, n], dev),
                remote(zs2.at[n, way], zs2r.at[n, way], t2_s.at[way, n], t2_r.at[way, n], dev))

    def peak(a):
        return jnp.maximum(jnp.max(jnp.max(jnp.abs(a), axis=0), axis=0, keepdims=True), TINY)

    def stage_a(n):
        take_halo(n + 1)
        diffuse(n)
        backward(n, 0, sib)
        share(n).start()
        backward(n, 1, own)

    def stage_b(n):
        share(n).wait_recv()
        for i in (0, 1, 3):
            own[n, i] = own[n, i] + sibr[n, i]
        far = own[n, 2] + sibr[n, 2]
        for way in range(2):
            if way == 0:
                a = jnp.concatenate([far[:HALF], own[n, 1, HALF:GLEV]], axis=0)
            else:
                a = jnp.concatenate([own[n, 3, 0:HALF], far[HALF:]], axis=0)
            top = peak(a)
            zs1[n, way] = top * (1.0 / 32767.0)
            zq1[n, way] = pack(a, top[None])
            each(first(n, way), "start")

    def stage_c(n):
        each(first(n, 0), "wait_recv")
        got = zq1r[n, 0].astype(F32) * zs1r[n, 0][None]
        a = own[n, 1, 0:HALF] + got[:HALF]
        top = peak(a)
        zs2[n, 0] = top * (1.0 / 32767.0)
        zqa[n] = pack(a, top[None])
        each(second(n, 0), "start")
        own[n, 0, HALF:GLEV] = own[n, 0, HALF:GLEV] + got[HALF:]
        each(first(n, 1), "wait_recv")
        got = zq1r[n, 1].astype(F32) * zs1r[n, 1][None]
        a = own[n, 3, HALF:GLEV] + got[HALF:]
        top = peak(a)
        zs2[n, 1] = top * (1.0 / 32767.0)
        zqb[n] = pack(a, top[None])
        each(second(n, 1), "start")
        own[n, 0, 0:HALF] = own[n, 0, 0:HALF] + got[:HALF]

    def stage_d(n):
        each(second(n, 0), "wait_recv")
        out_ref[0:HALF, chunk_rows(n), :] = own[n, 0, 0:HALF] + zqar[n].astype(F32) * zs2r[n, 0][None]
        each(second(n, 1), "wait_recv")
        out_ref[HALF:GLEV, chunk_rows(n), :] = own[n, 0, HALF:GLEV] + zqbr[n].astype(F32) * zs2r[n, 1][None]

    take_halo(0)

    def pipe(it, carry):
        pl.when(it < CHUNKS)(lambda: stage_a(it))
        pl.when(it > 0)(lambda: stage_b(it - 1))
        return carry

    def run(stage):
        def step(n, carry):
            stage(n)
            return carry
        lax.fori_loop(0, CHUNKS, step, 0)

    lax.fori_loop(0, CHUNKS + 1, pipe, 0)
    run(stage_c)
    run(stage_d)

    for j in range(1, GROUPS):
        send_modes(j).wait_send()

    @pl.when(has_next)
    def _():
        nu_up.wait_send()
        for i in range(MSGS):
            each(halo(i, 0), "wait_send")

    @pl.when(has_prev)
    def _():
        nu_down.wait_send()
        for i in range(MSGS):
            each(halo(i, 1), "wait_send")

    def sent(n):
        share(n).wait_send()
        for way in range(2):
            each(first(n, way), "wait_send")
            each(second(n, way), "wait_send")

    run(sent)


def tiles(a):
    lev = a.shape[0]
    return a.reshape(lev, ROWS, TILES, 128).transpose(0, 2, 1, 3).reshape(lev, TILES * ROWS, 128)


def untiles(a):
    lev = a.shape[0]
    return a.reshape(lev, TILES, ROWS, 128).transpose(0, 2, 1, 3).reshape(lev, ROWS, NLON)


def body(anomalies, vector, modes, order, weights, diffusivity):
    vmem, dma = pltpu.VMEM, pltpu.SemaphoreType.DMA
    hbm, smem = pl.BlockSpec(memory_space=pl.ANY), pl.BlockSpec(memory_space=pltpu.SMEM)
    rows = TILES * ROWS
    out = pl.pallas_call(
        kernel,
        out_shape=jax.ShapeDtypeStruct((GLEV, rows, 128), F32),
        in_specs=[hbm, hbm, hbm, smem, smem, hbm],
        out_specs=pl.BlockSpec(memory_space=pltpu.VMEM),
        scratch_shapes=[
            vmem((LEV, rows, 128), BF16),
            vmem((LEV, rows, 128), F32),
            vmem((2, LEV), F32),
            vmem((ROWS, NLON), F32),
            vmem((GROUPS, MODES, 256), F32),
            vmem((2, ROWS, NLON), F32),
            vmem((CHUNKS, LEV * 8, 256), BF16),
            vmem((CHUNKS, LEV * 8, 256), BF16),
            vmem((256, LEV * 8), BF16),
            vmem((2, 4 * LEV, 256), BF16),
            vmem((256, LEV * 8), BF16),
            vmem((2, 4 * LEV, 384), BF16),
            vmem((EXT, MODES, PADDED), F32),
            vmem((5, EXT - 2, 8, PADDED), F32),
            vmem((ROWS, MODES, WIDE), F32),
            vmem((384, 256), BF16),
            vmem((ROWS, MODES, PADDED), I16),
            vmem((1, PADDED), F32),
            vmem((2, ROWS, MODES, PADDED), I16),
            vmem((2, 1, PADDED), F32),
            vmem((CHUNKS, 4, GLEV, SUB, 128), F32),
            vmem((CHUNKS, 4, GLEV, SUB, 128), F32),
            vmem((CHUNKS, 4, GLEV, SUB, 128), F32),
            vmem((CHUNKS, 2, GLEV, SUB, 128), I16),
            vmem((CHUNKS, 2, 1, 128), F32),
            vmem((CHUNKS, 2, GLEV, SUB, 128), I16),
            vmem((CHUNKS, 2, 1, 128), F32),
            vmem((CHUNKS, HALF, SUB, 128), I16),
            vmem((CHUNKS, GLEV - HALF, SUB, 128), I16),
            vmem((CHUNKS, 2, 1, 128), F32),
            vmem((CHUNKS, HALF, SUB, 128), I16),
            vmem((CHUNKS, GLEV - HALF, SUB, 128), I16),
            vmem((CHUNKS, 2, 1, 128), F32),
            dma((2 + 2 * CHUNKS,)),
            dma((GROUPS,)), dma((GROUPS,)), dma((2,)), dma((2,)),
            dma((2, MSGS)), dma((2, MSGS)), dma((2, MSGS)), dma((2, MSGS)),
            dma((CHUNKS,)), dma((CHUNKS,)),
            dma((2, CHUNKS)), dma((2, CHUNKS)), dma((2, CHUNKS)), dma((2, CHUNKS)),
            dma((2, CHUNKS)), dma((2, CHUNKS)), dma((2, CHUNKS)), dma((2, CHUNKS)),
        ],
        compiler_params=pltpu.CompilerParams(
            collective_id=0, has_side_effects=True, vmem_limit_bytes=56 * 2**20),
    )(tiles(anomalies[0]), tiles(vector), modes, order, weights, diffusivity)
    return untiles(out)


def solution(mesh):
    return jax.shard_map(
        body,
        mesh=mesh,
        in_specs=(
            P("mode", None, "space", None),
            P(None, "space", None),
            P("mode", None),
            P(),
            P(),
            P("space", None),
        ),
        out_specs=P("mode", "space", None),
        check_vma=False,
    )
```

time: 213 us -> 50.6 us (0.24)
  waiting for transfers between devices: 135 us -> 0 us
  Pallas kernels: 0 us -> 47.8 us
  blocking collectives: 18.3 us -> 0 us
  matrix products: 15.6 us -> 0 us
  starting transfers between devices: 14.7 us -> 0 us
  between operations: 14.2 us -> 0.01 us
  local copies, waits for them, and re-layouts: 11.8 us -> 1.91 us
  other arithmetic: 3.09 us -> 0 us
    unnamed x2 -> x0, waiting for transfers between devices: 119 us -> none
    pallas_call x0 -> x1, Pallas kernels: none -> 47.8 us  [body(): pl.pallas_call(kernel, out_shape=jax.ShapeDtypeStruct((GLEV, rows, 128),...]
    all_gather x1 -> x0, blocking collectives: 18.3 us -> none  [body(): modes = lax.all_gather(modes, 'mode', axis=0, tiled=True)]
    ppermute x4 -> x0, waiting for transfers between devices: 16 us -> none  [the longest x2 8.34 us: extended(): lax.ppermute(head, axis, [((i + 1) % count, i) for i in range(ends)])]
    dot_general x2 -> x0, matrix products: 15.6 us -> none  [the longest x1 8.44 us: body(): jnp.einsum('kl,lan->kan', modes, xf * vector, precision=lax.Precision.HIG...]
    ppermute x4 -> x0, starting transfers between devices: 14.7 us -> none  [the longest x2 10.1 us: extended(): lax.ppermute(tail, axis, [(i, (i + 1) % count) for i in range(ends)])]
    mul x1 -> x0, local copies, waits for them, and re-layouts: 4.95 us -> none  [body(): weight * xf * back]
    unnamed x13 -> x1, local copies, waits for them, and re-layouts: 4.52 us -> 1.91 us
  transfers between devices with their start and end apart: 5 -> 0, of which waited for: 3 -> 0; matrix products, arithmetic and copies ran while one was open for 5% -> 0% of each run, Pallas kernels for 0% -> 0%
where the time goes in v2:
time: 50.6 us; the launch traced here: 49.7 us
  Pallas kernels  47.8 us (94%)
  local copies, waits for them, and re-layouts  1.91 us (4%)
    pallas_call x1, Pallas kernels, body(): pl.pallas_call(kernel, out_shape=jax.ShapeDtypeStruct((GLEV, rows, 128),...  47.8 us
    unnamed x1, local copies, waits for them, and re-layouts  1.91 us

profile of v2, /device:TPU:30, one launch (start us, length us, event | category | flops | bytes accessed | tf_op | source)
XLA Modules:
  0.0 49.7 jit_solution(415380058254383124)
XLA Ops:
  0.0 47.8 %shard_map.64 = f32[17,64,128]{2,1,0:T(8,128)} custom-call(bf16[136,64,128]{2,1,0:T(8,128)(2,1)} %bitcast.17, f32[136,64,128]{2,1,0:T(8,128)} %bitcast.15, f32[2,136]{1,0:T(2,128)} %modes_hbm.1, s32[8]{0:T(128)} %order_ref.1, f32[8]{0:T(128)} %weights_ref.1, f32[4,2048]{1,0:T(4,128)} %diff_hbm.1), custom_call_target="tpu_custom_call" | custom-call | tf_op jit(solution)/shard_map/pallas_call | solution.py:405
  47.8 1.9 %copy.11 = f32[17,4,2048]{2,1,0:T(4,128)} copy(f32[17,4,2048]{2,1,0:T(4,128)} %bitcast.16) | data formatting | bytes 1114112

commit v3 on v2

--- a/solution.py
+++ b/solution.py
@@ -29,10 +29,10 @@
     return jnp.round(a * (32767.0 / top)).astype(I16)
 
 
-def kernel(x_hbm, v_hbm, modes_hbm, order_ref, weights_ref, diff_hbm, out_ref,
-           xs, vs, mine, nu, mall, nuext, phi, plo, spread, pick, fwd, bwd, field, coef, loc, lcat,
+def kernel(x_hbm, v_hbm, modes_hbm, order_hbm, weights_hbm, diff_hbm, out_hbm,
+           order_ref, weights_ref, xs, vs, mine, nu, mall, nuext, phi, plo, spread, pick, fwd, bwd, field, face, loc, lcat,
            hq, hsc, hqr, hscr, sib, sibr, own, zq1, zs1, zq1r, zs1r, zqa, zqb, zs2, zqar, zqbr, zs2r,
-           lsem, m_s, m_r, d_s, d_r, hq_s, hq_r, hs_s, hs_r, sb_s, sb_r,
+           lsem, osem, m_s, m_r, d_s, d_r, hq_s, hq_r, hs_s, hs_r, sb_s, sb_r,
            z1_s, z1_r, t1_s, t1_r, z2_s, z2_r, t2_s, t2_r):
     me = lax.axis_index("mode")
     place = lax.axis_index("space")
@@ -61,8 +61,10 @@
     def get_v(n):
         return pltpu.make_async_copy(v_hbm.at[:, chunk_rows(n)], vs.at[:, chunk_rows(n)], lsem.at[2 + CHUNKS + n])
 
-    get_modes.start()
-    get_nu.start()
+    get_order = pltpu.make_async_copy(order_hbm, order_ref, lsem.at[2 + 2 * CHUNKS])
+    get_weights = pltpu.make_async_copy(weights_hbm, weights_ref, lsem.at[3 + 2 * CHUNKS])
+    for copy in (get_modes, get_nu, get_order, get_weights):
+        copy.start()
     for n in range(CHUNKS):
         get_x(n).start()
         get_v(n).start()
@@ -79,6 +81,42 @@
 
     lane_level = lax.broadcasted_iota(jnp.int32, (256, LEV * 8), 1) >> 3
     spread[...] = jnp.where(lane_level == lax.broadcasted_iota(jnp.int32, (256, LEV * 8), 0), 1.0, 0.0).astype(BF16)
+    get_modes.wait()
+    mall[0] = mine[...]
+    get_nu.wait()
+    get_order.wait()
+    get_weights.wait()
+
+    def products(n):
+        get_x(n).wait()
+        get_v(n).wait()
+
+        for b in range(LEV // 8):
+            lev = slice(b * 8, b * 8 + 8)
+            p = xs[lev, chunk_rows(n), :].astype(F32) * vs[lev, chunk_rows(n), :]
+            for h in range(2):
+                hi, lo = split(p[:, 8 * h : 8 * h + 8, :].reshape(64, 128))
+                phi[n, b * 64 : b * 64 + 64, 128 * h : 128 * h + 128] = hi
+                plo[n, b * 64 : b * 64 + 64, 128 * h : 128 * h + 128] = lo
+
+    pl.semaphore_wait(barrier, GROUPS - 1 + has_prev.astype(jnp.int32) + has_next.astype(jnp.int32))
+
+    def send_modes(j):
+        return remote(mall.at[0], mall.at[j], m_s.at[j], m_r.at[j], {"mode": (me + j) % GROUPS})
+
+    for j in range(1, GROUPS):
+        send_modes(j).start()
+    nu_up = remote(nu, nuext.at[0], d_s.at[0], d_r.at[0], after)
+    nu_down = remote(nu, nuext.at[1], d_s.at[1], d_r.at[1], before)
+    pl.when(has_next)(lambda: nu_up.start())
+    pl.when(has_prev)(lambda: nu_down.start())
+
+    def run(stage):
+        def step(n, carry):
+            stage(n)
+            return carry
+        lax.fori_loop(0, CHUNKS, step, 0)
+
     for i in range(GROUPS):
         c = 1 - core if i < 4 else core
         group = ((ring + i) % 4) * 2 + c
@@ -86,49 +124,15 @@
         pick[i // 4, (i % 4) * LEV : (i % 4 + 1) * LEV, :] = jnp.where(
             lax.broadcasted_iota(jnp.int32, (LEV, 256), 1) == level, 1.0, 0.0).astype(BF16)
 
-    get_modes.wait()
-    which = lax.broadcasted_iota(jnp.int32, (MODES, LEV), 0) - 2 * me
-    block = jnp.where(which == 0, mine[0:1, :], jnp.where(which == 1, mine[1:2, :], 0.0))
-    mall[0] = jnp.concatenate([block, jnp.zeros((MODES, 256 - LEV), F32)], axis=1)
-    get_nu.wait()
-
-    def products(n):
-        get_x(n).wait()
-        get_v(n).wait()
-
-        def part(b, carry):
-            lev = pl.ds(b * 8, 8)
-            p = xs[lev, chunk_rows(n), :].astype(F32) * vs[lev, chunk_rows(n), :]
-            for h in range(2):
-                hi, lo = split(p[:, 8 * h : 8 * h + 8, :].reshape(64, 128))
-                at = pl.ds(pl.multiple_of(b * 64, 64), 64)
-                phi[n, at, 128 * h : 128 * h + 128] = hi
-                plo[n, at, 128 * h : 128 * h + 128] = lo
-            return carry
-
-        lax.fori_loop(0, LEV // 8, part, 0)
-
-    products(0)
-    pl.semaphore_wait(barrier, GROUPS - 1 + has_prev.astype(jnp.int32) + has_next.astype(jnp.int32))
-
-    def send_modes(j):
-        return remote(mall.at[0], mall.at[j], m_s.at[j], m_r.at[j], {"mode": (me + j) % GROUPS})
-
-    for j in range(1, GROUPS):
-        send_modes(j).start()
-    nu_up = remote(nu, nuext.at[0], d_s.at[0], d_r.at[0], after)
-    nu_down = remote(nu, nuext.at[1], d_s.at[1], d_r.at[1], before)
-    pl.when(has_next)(lambda: nu_up.start())
-    pl.when(has_prev)(lambda: nu_down.start())
-
-    for n in range(1, CHUNKS):
-        products(n)
+    run(products)
 
     for j in range(1, GROUPS):
         send_modes(j).wait_recv()
-    modes = mall[0]
-    for j in range(1, GROUPS):
-        modes = modes + mall[j]
+    modes = jnp.zeros((MODES, LEV), F32)
+    for j in range(GROUPS):
+        row = lax.broadcasted_iota(jnp.int32, (MODES, LEV), 0) - 2 * ((me - j + GROUPS) % GROUPS)
+        modes = jnp.where(row == 0, mall[j, 0:1, :], jnp.where(row == 1, mall[j, 1:2, :], modes))
+    modes = jnp.concatenate([modes, jnp.zeros((MODES, 256 - LEV), F32)], axis=1)
     modes_hi, modes_lo = split(modes)
 
     both = jnp.dot(jnp.concatenate([modes_hi, modes_lo], axis=0), spread[...], preferred_element_type=F32)
@@ -137,6 +141,9 @@
         rows = both[half * MODES : (half + 1) * MODES]
         for q in range(8):
             fwd[half * 128 + q * MODES : half * 128 + (q + 1) * MODES, :] = jnp.where(sub == q, rows, 0.0).astype(BF16)
+
+    def peak(a):
+        return jnp.maximum(jnp.max(jnp.max(jnp.abs(a), axis=0), axis=0, keepdims=True), TINY)
 
     def project(n):
         main = jnp.dot(fwd[...], phi[n], preferred_element_type=F32)
@@ -149,11 +156,6 @@
                     q = (par * ROWS + r) * MODES
                     field[DIFF + r, :, at : at + 128] = total[q : q + MODES, h * 128 : h * 128 + 128]
 
-    for n in range(CHUNKS):
-        project(n)
-    field[DIFF : DIFF + ROWS, :, 0:128] = field[DIFF : DIFF + ROWS, :, NLON : NLON + 128]
-    field[DIFF : DIFF + ROWS, :, NLON + 128 : PADDED] = field[DIFF : DIFF + ROWS, :, 128:256]
-
     def halo_lanes(i):
         if isinstance(i, int) and i == 0:
             return pl.ds(0, 256)
@@ -169,14 +171,26 @@
         for copy in copies:
             getattr(copy, what)()
 
-    for i in range(MSGS):
+    def send_halo(i):
         lanes = halo_lanes(i)
         u = field[DIFF : DIFF + ROWS, :, lanes]
-        top = jnp.maximum(jnp.max(jnp.max(jnp.abs(u), axis=0), axis=0, keepdims=True), TINY)
+        top = peak(u)
         hsc[:, lanes] = top * (1.0 / 32767.0)
         hq[:, :, lanes] = pack(u, top[None])
         pl.when(has_next)(lambda: each(halo(i, 0), "start"))
         pl.when(has_prev)(lambda: each(halo(i, 1), "start"))
+
+    own_rows = slice(DIFF, DIFF + ROWS)
+    project(3)
+    field[own_rows, :, 0:128] = field[own_rows, :, NLON : NLON + 128]
+    project(0)
+    field[own_rows, :, NLON + 128 : PADDED] = field[own_rows, :, 128:256]
+    send_halo(0)
+    project(1)
+    send_halo(1)
+    project(2)
+    for i in range(2, MSGS):
+        send_halo(i)
 
     rep_hi = jnp.concatenate([modes_hi] * 8, axis=0)
     rep_lo = jnp.concatenate([modes_lo] * 8, axis=0)
@@ -213,19 +227,13 @@
         r = a % ROWS
         return jnp.broadcast_to(src[r : r + 1, :], (8, NLON))
 
-    top_mask, low_mask = has_prev.astype(F32), has_next.astype(F32)
-    for a in range(1, EXT - 1):
+    for a in range(EXT - 1):
         here = nu_row(a)
-        mask = top_mask if a < DIFF else low_mask if a >= DIFF + ROWS else None
-        arms = [0.5 * (here + other) for other in (
-            nu_row(a - 1), nu_row(a + 1), pltpu.roll(here, NLON - 1, 1), pltpu.roll(here, 1, 1))]
-        arms.append(1.0 - (arms[0] + arms[1] + arms[2] + arms[3]))
-        for c, arm in enumerate(arms):
-            if mask is not None:
-                arm = arm * mask
-            coef[c, a - 1, :, 128 : NLON + 128] = arm
-            coef[c, a - 1, :, 0:128] = arm[:, NLON - 128 : NLON]
-            coef[c, a - 1, :, NLON + 128 : PADDED] = arm[:, 0:128]
+        for c, other in enumerate((pltpu.roll(here, NLON - 1, 1), nu_row(a + 1))):
+            arm = 0.5 * (here + other)
+            face[c, a, :, 128 : NLON + 128] = arm
+            face[c, a, :, 0:128] = arm[:, NLON - 128 : NLON]
+            face[c, a, :, NLON + 128 : PADDED] = arm[:, 0:128]
 
     weight = jnp.float32(0.0)
     for s in range(GROUPS):
@@ -245,24 +253,32 @@
             field[DIFF + ROWS : EXT, :, lanes] = hqr[1, :, :, lanes].astype(F32) * hscr[1, :, lanes][None]
 
     window = WIDE + 256
+    top_mask, low_mask = has_prev.astype(F32), has_next.astype(F32)
 
     def diffuse(n):
         lanes = pl.ds(pl.multiple_of(n * WIDE, 128), window)
-        for kh in range(2):
-            u = [field[a, kh * 8 : kh * 8 + 8, lanes] for a in range(EXT)]
-            for s in range(1, DIFF + 1):
-                new = []
-                for a in range(s, EXT - s):
-                    c, up, down = u[a - s + 1], u[a - s], u[a - s + 2]
-                    new.append(
-                        coef[4, a - 1, :, lanes] * c
-                        + coef[0, a - 1, :, lanes] * up
-                        + coef[1, a - 1, :, lanes] * down
-                        + coef[2, a - 1, :, lanes] * pltpu.roll(c, window - 1, 1)
-                        + coef[3, a - 1, :, lanes] * pltpu.roll(c, 1, 1))
-                u = new
-            for r in range(ROWS):
-                loc[r, kh * 8 : kh * 8 + 8, :] = weight * u[r][:, 128 : 128 + WIDE]
+        def both_halves(c, a):
+            arm = face[c, a, :, lanes]
+            return jnp.concatenate([arm, arm], axis=0)
+
+        u = [field[a, :, lanes] for a in range(EXT)]
+        for s in range(1, DIFF + 1):
+            new = []
+            north = both_halves(1, s - 1) * (u[1] - u[0])
+            for a in range(s, EXT - s):
+                c, down = u[a - s + 1], u[a - s + 2]
+                south = both_halves(1, a) * (down - c)
+                east = both_halves(0, a) * (pltpu.roll(c, window - 1, 1) - c)
+                total = c + (south - north) + (east - pltpu.roll(east, 1, 1))
+                if a < DIFF:
+                    total = total * top_mask
+                elif a >= DIFF + ROWS:
+                    total = total * low_mask
+                new.append(total)
+                north = south
+            u = new
+        for r in range(ROWS):
+            loc[r] = weight * u[r][:, 128 : 128 + WIDE]
         for par in range(2):
             for r in range(ROWS):
                 q = (par * ROWS + r) * MODES
@@ -274,18 +290,20 @@
                     lcat[128 + q : 128 + q + MODES, cols] = lo
                     lcat[256 + q : 256 + q + MODES, cols] = hi
 
+    def share(n, i):
+        return remote(sib.at[n, i], sibr.at[n, i], sb_s.at[n, i], sb_r.at[n, i], partner)
+
     def backward(n, part, dst):
         back = jnp.dot(bwd[part], lcat[...], preferred_element_type=F32)
         c = core if part else 1 - core
-        for i in range(4):
+        for i in (2, 1, 3, 0):
             group = ((ring + i) % 4) * 2 + c
             xg = xs[pl.ds(group * GLEV, GLEV), chunk_rows(n), :].astype(F32)
             for h in range(2):
                 b = back[i * LEV : (i + 1) * LEV, h * 128 : h * 128 + 128].reshape(GLEV, 8, 128)
                 dst[n, i, :, 8 * h : 8 * h + 8, :] = xg[:, 8 * h : 8 * h + 8, :] * b
-
-    def share(n):
-        return remote(sib.at[n], sibr.at[n], sb_s.at[n], sb_r.at[n], partner)
+            if part == 0:
+                share(n, i).start()
 
     def first(n, way):
         dev = right if way == 0 else left
@@ -298,22 +316,19 @@
         return (remote(src.at[n], dst.at[n], z2_s.at[way, n], z2_r.at[way, n], dev),
                 remote(zs2.at[n, way], zs2r.at[n, way], t2_s.at[way, n], t2_r.at[way, n], dev))
 
-    def peak(a):
-        return jnp.maximum(jnp.max(jnp.max(jnp.abs(a), axis=0), axis=0, keepdims=True), TINY)
-
     def stage_a(n):
         take_halo(n + 1)
         diffuse(n)
         backward(n, 0, sib)
-        share(n).start()
         backward(n, 1, own)
 
     def stage_b(n):
-        share(n).wait_recv()
-        for i in (0, 1, 3):
-            own[n, i] = own[n, i] + sibr[n, i]
+        share(n, 2).wait_recv()
         far = own[n, 2] + sibr[n, 2]
         for way in range(2):
+            i = 1 if way == 0 else 3
+            share(n, i).wait_recv()
+            own[n, i] = own[n, i] + sibr[n, i]
             if way == 0:
                 a = jnp.concatenate([far[:HALF], own[n, 1, HALF:GLEV]], axis=0)
             else:
@@ -322,6 +337,8 @@
             zs1[n, way] = top * (1.0 / 32767.0)
             zq1[n, way] = pack(a, top[None])
             each(first(n, way), "start")
+        share(n, 0).wait_recv()
+        own[n, 0] = own[n, 0] + sibr[n, 0]
 
     def stage_c(n):
         each(first(n, 0), "wait_recv")
@@ -343,22 +360,21 @@
 
     def stage_d(n):
         each(second(n, 0), "wait_recv")
-        out_ref[0:HALF, chunk_rows(n), :] = own[n, 0, 0:HALF] + zqar[n].astype(F32) * zs2r[n, 0][None]
+        own[n, 0, 0:HALF] = own[n, 0, 0:HALF] + zqar[n].astype(F32) * zs2r[n, 0][None]
         each(second(n, 1), "wait_recv")
-        out_ref[HALF:GLEV, chunk_rows(n), :] = own[n, 0, HALF:GLEV] + zqbr[n].astype(F32) * zs2r[n, 1][None]
+        own[n, 0, HALF:GLEV] = own[n, 0, HALF:GLEV] + zqbr[n].astype(F32) * zs2r[n, 1][None]
+
+        put(n).start()
+
+    def put(n):
+        return pltpu.make_async_copy(own.at[n, 0], out_hbm.at[:, chunk_rows(n)], osem.at[n])
 
     take_halo(0)
 
     def pipe(it, carry):
         pl.when(it < CHUNKS)(lambda: stage_a(it))
-        pl.when(it > 0)(lambda: stage_b(it - 1))
+        pl.when(it != 1)(lambda: stage_b(jnp.maximum(it - 1, 0)))
         return carry
-
-    def run(stage):
-        def step(n, carry):
-            stage(n)
-            return carry
-        lax.fori_loop(0, CHUNKS, step, 0)
 
     lax.fori_loop(0, CHUNKS + 1, pipe, 0)
     run(stage_c)
@@ -380,7 +396,9 @@
             each(halo(i, 1), "wait_send")
 
     def sent(n):
-        share(n).wait_send()
+        for i in range(4):
+            share(n, i).wait_send()
+        put(n).wait()
         for way in range(2):
             each(first(n, way), "wait_send")
             each(second(n, way), "wait_send")
@@ -400,19 +418,21 @@
 
 def body(anomalies, vector, modes, order, weights, diffusivity):
     vmem, dma = pltpu.VMEM, pltpu.SemaphoreType.DMA
-    hbm, smem = pl.BlockSpec(memory_space=pl.ANY), pl.BlockSpec(memory_space=pltpu.SMEM)
+    hbm = pl.BlockSpec(memory_space=pltpu.HBM)
     rows = TILES * ROWS
     out = pl.pallas_call(
         kernel,
         out_shape=jax.ShapeDtypeStruct((GLEV, rows, 128), F32),
-        in_specs=[hbm, hbm, hbm, smem, smem, hbm],
-        out_specs=pl.BlockSpec(memory_space=pltpu.VMEM),
+        in_specs=[hbm] * 6,
+        out_specs=pl.BlockSpec(memory_space=pl.ANY),
         scratch_shapes=[
+            pltpu.SMEM((GROUPS,), jnp.int32),
+            pltpu.SMEM((GROUPS,), F32),
             vmem((LEV, rows, 128), BF16),
             vmem((LEV, rows, 128), F32),
             vmem((2, LEV), F32),
             vmem((ROWS, NLON), F32),
-            vmem((GROUPS, MODES, 256), F32),
+            vmem((GROUPS, 2, LEV), F32),
             vmem((2, ROWS, NLON), F32),
             vmem((CHUNKS, LEV * 8, 256), BF16),
             vmem((CHUNKS, LEV * 8, 256), BF16),
@@ -421,7 +441,7 @@
             vmem((256, LEV * 8), BF16),
             vmem((2, 4 * LEV, 384), BF16),
             vmem((EXT, MODES, PADDED), F32),
-            vmem((5, EXT - 2, 8, PADDED), F32),
+            vmem((2, EXT - 1, 8, PADDED), F32),
             vmem((ROWS, MODES, WIDE), F32),
             vmem((384, 256), BF16),
             vmem((ROWS, MODES, PADDED), I16),
@@ -441,16 +461,16 @@
             vmem((CHUNKS, HALF, SUB, 128), I16),
             vmem((CHUNKS, GLEV - HALF, SUB, 128), I16),
             vmem((CHUNKS, 2, 1, 128), F32),
-            dma((2 + 2 * CHUNKS,)),
+            dma((4 + 2 * CHUNKS,)), dma((CHUNKS,)),
             dma((GROUPS,)), dma((GROUPS,)), dma((2,)), dma((2,)),
             dma((2, MSGS)), dma((2, MSGS)), dma((2, MSGS)), dma((2, MSGS)),
-            dma((CHUNKS,)), dma((CHUNKS,)),
+            dma((CHUNKS, 4)), dma((CHUNKS, 4)),
             dma((2, CHUNKS)), dma((2, CHUNKS)), dma((2, CHUNKS)), dma((2, CHUNKS)),
             dma((2, CHUNKS)), dma((2, CHUNKS)), dma((2, CHUNKS)), dma((2, CHUNKS)),
         ],
         compiler_params=pltpu.CompilerParams(
-            collective_id=0, has_side_effects=True, vmem_limit_bytes=56 * 2**20),
-    )(tiles(anomalies[0]), tiles(vector), modes, order, weights, diffusivity)
+            collective_id=0, has_side_effects=True, vmem_limit_bytes=53 * 2**20),
+    )(*[pltpu.with_memory_space_constraint(a, pltpu.HBM) for a in (tiles(anomalies[0]), tiles(vector), modes, order, weights, diffusivity)])
     return untiles(out)
 
 

time: 50.6 us -> 46.4 us (0.917)
  Pallas kernels: 47.8 us -> 44.9 us
  local copies, waits for them, and re-layouts: 1.91 us -> 0.81 us
    pallas_call x1, Pallas kernels: 47.8 us -> 44.9 us  [body(): pl.pallas_call(kernel, out_shape=jax.ShapeDtypeStruct((GLEV, rows, 128),...]
    unnamed x1, local copies, waits for them, and re-layouts: 1.91 us -> 0.81 us
where the time goes in v3:
time: 46.4 us; the launch traced here: 45.7 us
  Pallas kernels  44.9 us (97%)
  local copies, waits for them, and re-layouts  0.81 us (2%)
    pallas_call x1, Pallas kernels, body(): pl.pallas_call(kernel, out_shape=jax.ShapeDtypeStruct((GLEV, rows, 128),...  44.9 us

profile of v3, /device:TPU:30, one launch (start us, length us, event | category | flops | bytes accessed | tf_op | source)
XLA Modules:
  0.0 45.7 jit_solution(8647288810681950927)
XLA Ops:
  0.0 44.9 %shard_map.64 = f32[17,64,128]{2,1,0:T(8,128)S(1)} custom-call(bf16[136,64,128]{2,1,0:T(8,128)(2,1)} %bitcast.17, f32[136,64,128]{2,1,0:T(8,128)} %bitcast.16, f32[2,136]{1,0:T(2,128)} %modes_hbm.1, s32[8]{0:T(128)} %order_hbm.1, f32[8]{0:T(128)} %weights_hbm.1, f32[4,2048]{1,0:T(4,128)} %diff_hbm.1), custom_call_target="tpu_custom_call" | custom-call | tf_op jit(solution)/shard_map/pallas_call | solution.py:423
  44.9 0.8 %copy.11 = f32[17,4,2048]{2,1,0:T(4,128)} copy(f32[17,4,2048]{2,1,0:T(4,128)S(1)} %bitcast.15) | data formatting | bytes 1114112

commit v4 on v3

--- a/solution.py
+++ b/solution.py
@@ -31,8 +31,8 @@
 
 def kernel(x_hbm, v_hbm, modes_hbm, order_hbm, weights_hbm, diff_hbm, out_hbm,
            order_ref, weights_ref, xs, vs, mine, nu, mall, nuext, phi, plo, spread, pick, fwd, bwd, field, face, loc, lcat,
-           hq, hsc, hqr, hscr, sib, sibr, own, zq1, zs1, zq1r, zs1r, zqa, zqb, zs2, zqar, zqbr, zs2r,
-           lsem, osem, m_s, m_r, d_s, d_r, hq_s, hq_r, hs_s, hs_r, sb_s, sb_r,
+           hq, hsc, hqr, hscr, xsib, lsib, own, zq1, zs1, zq1r, zs1r, zqa, zqb, zs2, zqar, zqbr, zs2r,
+           lsem, osem, m_s, m_r, d_s, d_r, hq_s, hq_r, hs_s, hs_r, sb_s, sb_r, xb_s, xb_r,
            z1_s, z1_r, t1_s, t1_r, z2_s, z2_r, t2_s, t2_r):
     me = lax.axis_index("mode")
     place = lax.axis_index("space")
@@ -117,14 +117,21 @@
             return carry
         lax.fori_loop(0, CHUNKS, step, 0)
 
-    for i in range(GROUPS):
-        c = 1 - core if i < 4 else core
-        group = ((ring + i) % 4) * 2 + c
-        level = group * GLEV + (lax.broadcasted_iota(jnp.int32, (LEV, 256), 0) >> 3)
-        pick[i // 4, (i % 4) * LEV : (i % 4 + 1) * LEV, :] = jnp.where(
+    def levels_of(i, c):
+        return pl.ds((((ring + i) % 4) * 2 + c) * GLEV, GLEV)
+
+    for i in range(4):
+        level = (((ring + i) % 4) * 2 + core) * GLEV + (lax.broadcasted_iota(jnp.int32, (LEV, 256), 0) >> 3)
+        pick[i * LEV : (i + 1) * LEV, :] = jnp.where(
             lax.broadcasted_iota(jnp.int32, (LEV, 256), 1) == level, 1.0, 0.0).astype(BF16)
 
     run(products)
+
+    def lend(i):
+        return remote(xs.at[levels_of(i, 1 - core)], xsib.at[i], xb_s.at[i], xb_r.at[i], partner)
+
+    for i in range(4):
+        lend(i).start()
 
     for j in range(1, GROUPS):
         send_modes(j).wait_recv()
@@ -196,13 +203,11 @@
     rep_lo = jnp.concatenate([modes_lo] * 8, axis=0)
     same = (lax.broadcasted_iota(jnp.int32, (4 * LEV, 128), 0) & 7) == (lax.broadcasted_iota(jnp.int32, (4 * LEV, 128), 1) >> 4)
     last = (((1,), (1,)), ((), ()))
-    for part in range(2):
-        hi = lax.dot_general(pick[part], rep_hi, last, preferred_element_type=F32)
-        lo = lax.dot_general(pick[part], rep_lo, last, preferred_element_type=F32)
-        hi = jnp.where(same, hi, 0.0).astype(BF16)
-        bwd[part, :, 0:128] = hi
-        bwd[part, :, 128:256] = hi
-        bwd[part, :, 256:384] = jnp.where(same, lo, 0.0).astype(BF16)
+    hi = jnp.where(same, lax.dot_general(pick[...], rep_hi, last, preferred_element_type=F32), 0.0).astype(BF16)
+    bwd[:, 0:128] = hi
+    bwd[:, 128:256] = hi
+    lo = lax.dot_general(pick[...], rep_lo, last, preferred_element_type=F32)
+    bwd[:, 256:384] = jnp.where(same, lo, 0.0).astype(BF16)
 
     @pl.when(has_prev)
     def _():
@@ -286,24 +291,20 @@
                     t = (2 * h + par) * 128
                     hi, lo = split(loc[r, :, t : t + 128])
                     cols = slice(h * 128, h * 128 + 128)
-                    lcat[q : q + MODES, cols] = hi
-                    lcat[128 + q : 128 + q + MODES, cols] = lo
-                    lcat[256 + q : 256 + q + MODES, cols] = hi
-
-    def share(n, i):
-        return remote(sib.at[n, i], sibr.at[n, i], sb_s.at[n, i], sb_r.at[n, i], partner)
-
-    def backward(n, part, dst):
-        back = jnp.dot(bwd[part], lcat[...], preferred_element_type=F32)
-        c = core if part else 1 - core
-        for i in (2, 1, 3, 0):
-            group = ((ring + i) % 4) * 2 + c
-            xg = xs[pl.ds(group * GLEV, GLEV), chunk_rows(n), :].astype(F32)
-            for h in range(2):
-                b = back[i * LEV : (i + 1) * LEV, h * 128 : h * 128 + 128].reshape(GLEV, 8, 128)
-                dst[n, i, :, 8 * h : 8 * h + 8, :] = xg[:, 8 * h : 8 * h + 8, :] * b
-            if part == 0:
-                share(n, i).start()
+                    lcat[n, q : q + MODES, cols] = hi
+                    lcat[n, 128 + q : 128 + q + MODES, cols] = lo
+
+    def share(n):
+        return remote(lcat.at[n], lsib.at[n], sb_s.at[n], sb_r.at[n], partner)
+
+    def backward(terms):
+        return (jnp.dot(bwd[:, 0:256], terms[...], preferred_element_type=F32)
+                + jnp.dot(bwd[:, 256:384], terms[0:128, :], preferred_element_type=F32))
+
+    def times(back, i, x):
+        return jnp.concatenate(
+            [x[:, 8 * h : 8 * h + 8, :] * back[i * LEV : (i + 1) * LEV, h * 128 : h * 128 + 128].reshape(GLEV, 8, 128)
+             for h in range(2)], axis=1)
 
     def first(n, way):
         dev = right if way == 0 else left
@@ -319,26 +320,32 @@
     def stage_a(n):
         take_halo(n + 1)
         diffuse(n)
-        backward(n, 0, sib)
-        backward(n, 1, own)
+        share(n).start()
+        back = backward(lcat.at[n])
+        for i in range(4):
+            own[n, i] = times(back, i, xs[levels_of(i, core), chunk_rows(n), :].astype(F32))
 
     def stage_b(n):
-        share(n, 2).wait_recv()
-        far = own[n, 2] + sibr[n, 2]
+        share(n).wait_recv()
+        back = backward(lsib.at[n])
+
+        def both(i):
+            return own[n, i] + times(back, i, xsib[i, :, chunk_rows(n), :].astype(F32))
+
+        far = both(2)
         for way in range(2):
             i = 1 if way == 0 else 3
-            share(n, i).wait_recv()
-            own[n, i] = own[n, i] + sibr[n, i]
+            near = both(i)
+            own[n, i] = near
             if way == 0:
-                a = jnp.concatenate([far[:HALF], own[n, 1, HALF:GLEV]], axis=0)
+                a = jnp.concatenate([far[:HALF], near[HALF:GLEV]], axis=0)
             else:
-                a = jnp.concatenate([own[n, 3, 0:HALF], far[HALF:]], axis=0)
+                a = jnp.concatenate([near[0:HALF], far[HALF:]], axis=0)
             top = peak(a)
             zs1[n, way] = top * (1.0 / 32767.0)
             zq1[n, way] = pack(a, top[None])
             each(first(n, way), "start")
-        share(n, 0).wait_recv()
-        own[n, 0] = own[n, 0] + sibr[n, 0]
+        own[n, 0] = both(0)
 
     def stage_c(n):
         each(first(n, 0), "wait_recv")
@@ -370,6 +377,8 @@
         return pltpu.make_async_copy(own.at[n, 0], out_hbm.at[:, chunk_rows(n)], osem.at[n])
 
     take_halo(0)
+    for i in range(4):
+        lend(i).wait_recv()
 
     def pipe(it, carry):
         pl.when(it < CHUNKS)(lambda: stage_a(it))
@@ -382,6 +391,8 @@
 
     for j in range(1, GROUPS):
         send_modes(j).wait_send()
+    for i in range(4):
+        lend(i).wait_send()
 
     @pl.when(has_next)
     def _():
@@ -396,8 +407,7 @@
             each(halo(i, 1), "wait_send")
 
     def sent(n):
-        for i in range(4):
-            share(n, i).wait_send()
+        share(n).wait_send()
         put(n).wait()
         for way in range(2):
             each(first(n, way), "wait_send")
@@ -437,19 +447,19 @@
             vmem((CHUNKS, LEV * 8, 256), BF16),
             vmem((CHUNKS, LEV * 8, 256), BF16),
             vmem((256, LEV * 8), BF16),
-            vmem((2, 4 * LEV, 256), BF16),
+            vmem((4 * LEV, 256), BF16),
             vmem((256, LEV * 8), BF16),
-            vmem((2, 4 * LEV, 384), BF16),
+            vmem((4 * LEV, 384), BF16),
             vmem((EXT, MODES, PADDED), F32),
             vmem((2, EXT - 1, 8, PADDED), F32),
             vmem((ROWS, MODES, WIDE), F32),
-            vmem((384, 256), BF16),
+            vmem((CHUNKS, 256, 256), BF16),
             vmem((ROWS, MODES, PADDED), I16),
             vmem((1, PADDED), F32),
             vmem((2, ROWS, MODES, PADDED), I16),
             vmem((2, 1, PADDED), F32),
-            vmem((CHUNKS, 4, GLEV, SUB, 128), F32),
-            vmem((CHUNKS, 4, GLEV, SUB, 128), F32),
+            vmem((4, GLEV, rows, 128), BF16),
+            vmem((CHUNKS, 256, 256), BF16),
             vmem((CHUNKS, 4, GLEV, SUB, 128), F32),
             vmem((CHUNKS, 2, GLEV, SUB, 128), I16),
             vmem((CHUNKS, 2, 1, 128), F32),
@@ -464,7 +474,7 @@
             dma((4 + 2 * CHUNKS,)), dma((CHUNKS,)),
             dma((GROUPS,)), dma((GROUPS,)), dma((2,)), dma((2,)),
             dma((2, MSGS)), dma((2, MSGS)), dma((2, MSGS)), dma((2, MSGS)),
-            dma((CHUNKS, 4)), dma((CHUNKS, 4)),
+            dma((CHUNKS,)), dma((CHUNKS,)), dma((4,)), dma((4,)),
             dma((2, CHUNKS)), dma((2, CHUNKS)), dma((2, CHUNKS)), dma((2, CHUNKS)),
             dma((2, CHUNKS)), dma((2, CHUNKS)), dma((2, CHUNKS)), dma((2, CHUNKS)),
         ],

time: 46.4 us -> 46.6 us (level); the launches traced: 45.7 us -> 46.5 us
  Pallas kernels: 44.9 us -> 45.7 us
    pallas_call x1, Pallas kernels: 44.9 us -> 45.7 us  [body(): pl.pallas_call(kernel, out_shape=jax.ShapeDtypeStruct((GLEV, rows, 128),...]
where the time goes in v4:
time: 46.6 us; the launch traced here: 46.5 us
  Pallas kernels  45.7 us (98%)
  local copies, waits for them, and re-layouts  0.81 us (2%)
    pallas_call x1, Pallas kernels, body(): pl.pallas_call(kernel, out_shape=jax.ShapeDtypeStruct((GLEV, rows, 128),...  45.7 us

profile of v4, /device:TPU:30, one launch (start us, length us, event | category | flops | bytes accessed | tf_op | source)
XLA Modules:
  0.0 46.5 jit_solution(795726294419417430)
XLA Ops:
  0.0 45.7 %shard_map.64 = f32[17,64,128]{2,1,0:T(8,128)S(1)} custom-call(bf16[136,64,128]{2,1,0:T(8,128)(2,1)} %bitcast.17, f32[136,64,128]{2,1,0:T(8,128)} %bitcast.16, f32[2,136]{1,0:T(2,128)} %modes_hbm.1, s32[8]{0:T(128)} %order_hbm.1, f32[8]{0:T(128)} %weights_hbm.1, f32[4,2048]{1,0:T(4,128)} %diff_hbm.1), custom_call_target="tpu_custom_call" | custom-call | tf_op jit(solution)/shard_map/pallas_call | solution.py:433
  45.7 0.8 %copy.11 = f32[17,4,2048]{2,1,0:T(4,128)} copy(f32[17,4,2048]{2,1,0:T(4,128)S(1)} %bitcast.15) | data formatting | bytes 1114112

commit v5 on v4

--- a/solution.py
+++ b/solution.py
@@ -14,8 +14,10 @@
 WIDE = NLON // CHUNKS
 PADDED = NLON + 256
 EXT = ROWS + 2 * DIFF
-HALF = (GLEV + 1) // 2
+UP = (10, 4, 7, 13)
+FAR, NEAR, PAST = 0, 1, 2
 MSGS = CHUNKS + 1
+BY_DISTANCE = (4, 3, 5, 2, 6, 1, 7)
 TINY = 1e-33
 F32, BF16, I16 = jnp.float32, jnp.bfloat16, jnp.int16
 
@@ -29,11 +31,11 @@
     return jnp.round(a * (32767.0 / top)).astype(I16)
 
 
-def kernel(x_hbm, v_hbm, modes_hbm, order_hbm, weights_hbm, diff_hbm, out_hbm,
+def kernel(x_hbm, v_hbm, modes_hbm, order_hbm, weights_hbm, diff_hbm, out_ref,
            order_ref, weights_ref, xs, vs, mine, nu, mall, nuext, phi, plo, spread, pick, fwd, bwd, field, face, loc, lcat,
-           hq, hsc, hqr, hscr, xsib, lsib, own, zq1, zs1, zq1r, zs1r, zqa, zqb, zs2, zqar, zqbr, zs2r,
-           lsem, osem, m_s, m_r, d_s, d_r, hq_s, hq_r, hs_s, hs_r, sb_s, sb_r, xb_s, xb_r,
-           z1_s, z1_r, t1_s, t1_r, z2_s, z2_r, t2_s, t2_r):
+           hq, hsc, hqr, hscr, xsib, lsib, own, zf, zfr, zn, zp, zr, tf, tfr, tn, tnr, tp, tpr,
+           lsem, m_s, m_r, d_s, d_r, hq_s, hq_r, hs_s, hs_r, sb_s, sb_r, xb_s, xb_r,
+           z_s, z_r, t_s, t_r):
     me = lax.axis_index("mode")
     place = lax.axis_index("space")
     ring, core = me // 2, me % 2
@@ -49,6 +51,16 @@
             src_ref=src, dst_ref=dst, send_sem=ss, recv_sem=rs, device_id=dev,
             device_id_type=pl.DeviceIdType.MESH)
 
+    barrier = pltpu.get_barrier_semaphore()
+
+    def greet(dev):
+        pl.semaphore_signal(barrier, inc=1, device_id=dev, device_id_type=pl.DeviceIdType.MESH)
+
+    for j in BY_DISTANCE:
+        greet({"mode": (me + j) % GROUPS})
+    pl.when(has_prev)(lambda: greet(before))
+    pl.when(has_next)(lambda: greet(after))
+
     def chunk_rows(n):
         return pl.ds(pl.multiple_of(n * SUB, SUB), SUB)
 
@@ -69,16 +81,6 @@
         get_x(n).start()
         get_v(n).start()
 
-    barrier = pltpu.get_barrier_semaphore()
-
-    def greet(dev):
-        pl.semaphore_signal(barrier, inc=1, device_id=dev, device_id_type=pl.DeviceIdType.MESH)
-
-    for j in range(1, GROUPS):
-        greet({"mode": (me + j) % GROUPS})
-    pl.when(has_prev)(lambda: greet(before))
-    pl.when(has_next)(lambda: greet(after))
-
     lane_level = lax.broadcasted_iota(jnp.int32, (256, LEV * 8), 1) >> 3
     spread[...] = jnp.where(lane_level == lax.broadcasted_iota(jnp.int32, (256, LEV * 8), 0), 1.0, 0.0).astype(BF16)
     get_modes.wait()
@@ -104,7 +106,7 @@
     def send_modes(j):
         return remote(mall.at[0], mall.at[j], m_s.at[j], m_r.at[j], {"mode": (me + j) % GROUPS})
 
-    for j in range(1, GROUPS):
+    for j in BY_DISTANCE:
         send_modes(j).start()
     nu_up = remote(nu, nuext.at[0], d_s.at[0], d_r.at[0], after)
     nu_down = remote(nu, nuext.at[1], d_s.at[1], d_r.at[1], before)
@@ -129,9 +131,6 @@
 
     def lend(i):
         return remote(xs.at[levels_of(i, 1 - core)], xsib.at[i], xb_s.at[i], xb_r.at[i], partner)
-
-    for i in range(4):
-        lend(i).start()
 
     for j in range(1, GROUPS):
         send_modes(j).wait_recv()
@@ -198,6 +197,9 @@
     project(2)
     for i in range(2, MSGS):
         send_halo(i)
+
+    for i in range(4):
+        lend(i).start()
 
     rep_hi = jnp.concatenate([modes_hi] * 8, axis=0)
     rep_lo = jnp.concatenate([modes_lo] * 8, axis=0)
@@ -306,16 +308,38 @@
             [x[:, 8 * h : 8 * h + 8, :] * back[i * LEV : (i + 1) * LEV, h * 128 : h * 128 + 128].reshape(GLEV, 8, 128)
              for h in range(2)], axis=1)
 
-    def first(n, way):
+    def carry_sum(kind, n, way, c):
+        dest = (c + 2) % 4 if kind == FAR else (c + 1) % 4 if way == 0 else (c + 3) % 4
+        rising = (way == 0) == (kind != NEAR)
+        cut = slice(0, UP[dest]) if rising else slice(UP[dest], GLEV)
         dev = right if way == 0 else left
-        return (remote(zq1.at[n, way], zq1r.at[n, way], z1_s.at[way, n], z1_r.at[way, n], dev),
-                remote(zs1.at[n, way], zs1r.at[n, way], t1_s.at[way, n], t1_r.at[way, n], dev))
-
-    def second(n, way):
-        dev = right if way == 0 else left
-        src, dst = (zqa, zqar) if way == 0 else (zqb, zqbr)
-        return (remote(src.at[n], dst.at[n], z2_s.at[way, n], z2_r.at[way, n], dev),
-                remote(zs2.at[n, way], zs2r.at[n, way], t2_s.at[way, n], t2_r.at[way, n], dev))
+        if kind == FAR:
+            src, dst, one, two = zf.at[n, cut], zfr.at[n, way, cut], tf.at[n], tfr.at[n, way]
+        elif kind == NEAR:
+            src, dst, one, two = zn.at[n, way, cut], zr.at[n, way, cut], tn.at[n, way], tnr.at[n, way]
+        else:
+            src, dst, one, two = zp.at[n, way, cut], zr.at[n, way, cut], tp.at[n, way], tpr.at[n, way]
+        return (remote(src, dst, z_s.at[kind, way, n], z_r.at[kind, way, n], dev),
+                remote(one, two, t_s.at[kind, way, n], t_r.at[kind, way, n], dev))
+
+    def act(kind, n, way, what):
+        step = 0 if what != "wait_recv" else 3 if way == 0 else 1
+        for c in range(4):
+            pl.when(ring == c)(lambda c=c: each(carry_sum(kind, n, way, (c + step) % 4), what))
+
+    lev_index = lax.broadcasted_iota(jnp.int32, (GLEV, 1, 128), 0)
+
+    def rises(step):
+        dest = (ring + step) % 4
+        up = jnp.int32(UP[0])
+        for d in range(1, 4):
+            up = jnp.where(dest == d, UP[d], up)
+        return lev_index < up
+
+    def quantize(a, q, t):
+        top = peak(a)
+        t[...] = top * (1.0 / 32767.0)
+        q[...] = pack(a, top[None])
 
     def stage_a(n):
         take_halo(n + 1)
@@ -332,49 +356,38 @@
         def both(i):
             return own[n, i] + times(back, i, xsib[i, :, chunk_rows(n), :].astype(F32))
 
-        far = both(2)
+        quantize(both(2), zf.at[n], tf.at[n])
+        for way in range(2):
+            act(FAR, n, way, "start")
         for way in range(2):
             i = 1 if way == 0 else 3
-            near = both(i)
-            own[n, i] = near
-            if way == 0:
-                a = jnp.concatenate([far[:HALF], near[HALF:GLEV]], axis=0)
-            else:
-                a = jnp.concatenate([near[0:HALF], far[HALF:]], axis=0)
-            top = peak(a)
-            zs1[n, way] = top * (1.0 / 32767.0)
-            zq1[n, way] = pack(a, top[None])
-            each(first(n, way), "start")
+            own[n, i] = both(i)
+            quantize(own[n, i], zn.at[n, way], tn.at[n, way])
+        pl.when(n == 0)(lambda: start_near(n))
         own[n, 0] = both(0)
 
+    def start_near(n):
+        for way in range(2):
+            act(NEAR, n, way, "start")
+
     def stage_c(n):
-        each(first(n, 0), "wait_recv")
-        got = zq1r[n, 0].astype(F32) * zs1r[n, 0][None]
-        a = own[n, 1, 0:HALF] + got[:HALF]
-        top = peak(a)
-        zs2[n, 0] = top * (1.0 / 32767.0)
-        zqa[n] = pack(a, top[None])
-        each(second(n, 0), "start")
-        own[n, 0, HALF:GLEV] = own[n, 0, HALF:GLEV] + got[HALF:]
-        each(first(n, 1), "wait_recv")
-        got = zq1r[n, 1].astype(F32) * zs1r[n, 1][None]
-        a = own[n, 3, HALF:GLEV] + got[HALF:]
-        top = peak(a)
-        zs2[n, 1] = top * (1.0 / 32767.0)
-        zqb[n] = pack(a, top[None])
-        each(second(n, 1), "start")
-        own[n, 0, 0:HALF] = own[n, 0, 0:HALF] + got[:HALF]
+        for way in range(2):
+            act(FAR, n, way, "wait_recv")
+            got = own[n, 1 if way == 0 else 3] + zfr[n, way].astype(F32) * tfr[n, way][None]
+            up = rises(1 if way == 0 else 3)
+            a = jnp.where(up, got, 0.0) if way == 0 else jnp.where(up, 0.0, got)
+            quantize(a, zp.at[n, way], tp.at[n, way])
+            act(PAST, n, way, "start")
 
     def stage_d(n):
-        each(second(n, 0), "wait_recv")
-        own[n, 0, 0:HALF] = own[n, 0, 0:HALF] + zqar[n].astype(F32) * zs2r[n, 0][None]
-        each(second(n, 1), "wait_recv")
-        own[n, 0, HALF:GLEV] = own[n, 0, HALF:GLEV] + zqbr[n].astype(F32) * zs2r[n, 1][None]
-
-        put(n).start()
-
-    def put(n):
-        return pltpu.make_async_copy(own.at[n, 0], out_hbm.at[:, chunk_rows(n)], osem.at[n])
+        total = own[n, 0]
+        up = rises(0)
+        for way in range(2):
+            act(NEAR, n, way, "wait_recv")
+            act(PAST, n, way, "wait_recv")
+            scale = jnp.where(up if way == 0 else jnp.logical_not(up), tpr[n, way][None], tnr[n, way][None])
+            total = total + zr[n, way].astype(F32) * scale
+        out_ref[:, chunk_rows(n), :] = total
 
     take_halo(0)
     for i in range(4):
@@ -385,7 +398,12 @@
         pl.when(it != 1)(lambda: stage_b(jnp.maximum(it - 1, 0)))
         return carry
 
+    def later_near(n, carry):
+        start_near(n)
+        return carry
+
     lax.fori_loop(0, CHUNKS + 1, pipe, 0)
+    lax.fori_loop(1, CHUNKS, later_near, 0)
     run(stage_c)
     run(stage_d)
 
@@ -408,10 +426,9 @@
 
     def sent(n):
         share(n).wait_send()
-        put(n).wait()
         for way in range(2):
-            each(first(n, way), "wait_send")
-            each(second(n, way), "wait_send")
+            for kind in (FAR, NEAR, PAST):
+                act(kind, n, way, "wait_send")
 
     run(sent)
 
@@ -434,7 +451,7 @@
         kernel,
         out_shape=jax.ShapeDtypeStruct((GLEV, rows, 128), F32),
         in_specs=[hbm] * 6,
-        out_specs=pl.BlockSpec(memory_space=pl.ANY),
+        out_specs=pl.BlockSpec(memory_space=pltpu.VMEM),
         scratch_shapes=[
             pltpu.SMEM((GROUPS,), jnp.int32),
             pltpu.SMEM((GROUPS,), F32),
@@ -461,22 +478,22 @@
             vmem((4, GLEV, rows, 128), BF16),
             vmem((CHUNKS, 256, 256), BF16),
             vmem((CHUNKS, 4, GLEV, SUB, 128), F32),
+            vmem((CHUNKS, GLEV, SUB, 128), I16),
             vmem((CHUNKS, 2, GLEV, SUB, 128), I16),
+            vmem((CHUNKS, 2, GLEV, SUB, 128), I16),
+            vmem((CHUNKS, 2, GLEV, SUB, 128), I16),
+            vmem((CHUNKS, 2, GLEV, SUB, 128), I16),
+            vmem((CHUNKS, 1, 128), F32),
             vmem((CHUNKS, 2, 1, 128), F32),
-            vmem((CHUNKS, 2, GLEV, SUB, 128), I16),
             vmem((CHUNKS, 2, 1, 128), F32),
-            vmem((CHUNKS, HALF, SUB, 128), I16),
-            vmem((CHUNKS, GLEV - HALF, SUB, 128), I16),
             vmem((CHUNKS, 2, 1, 128), F32),
-            vmem((CHUNKS, HALF, SUB, 128), I16),
-            vmem((CHUNKS, GLEV - HALF, SUB, 128), I16),
             vmem((CHUNKS, 2, 1, 128), F32),
-            dma((4 + 2 * CHUNKS,)), dma((CHUNKS,)),
+            vmem((CHUNKS, 2, 1, 128), F32),
+            dma((4 + 2 * CHUNKS,)),
             dma((GROUPS,)), dma((GROUPS,)), dma((2,)), dma((2,)),
             dma((2, MSGS)), dma((2, MSGS)), dma((2, MSGS)), dma((2, MSGS)),
             dma((CHUNKS,)), dma((CHUNKS,)), dma((4,)), dma((4,)),
-            dma((2, CHUNKS)), dma((2, CHUNKS)), dma((2, CHUNKS)), dma((2, CHUNKS)),
-            dma((2, CHUNKS)), dma((2, CHUNKS)), dma((2, CHUNKS)), dma((2, CHUNKS)),
+            dma((3, 2, CHUNKS)), dma((3, 2, CHUNKS)), dma((3, 2, CHUNKS)), dma((3, 2, CHUNKS)),
         ],
         compiler_params=pltpu.CompilerParams(
             collective_id=0, has_side_effects=True, vmem_limit_bytes=53 * 2**20),

time: 46.6 us -> 45.2 us (0.970)
  Pallas kernels: 45.7 us -> 44.1 us
    pallas_call x1, Pallas kernels: 45.7 us -> 44.1 us  [body(): pl.pallas_call(kernel, out_shape=jax.ShapeDtypeStruct((GLEV, rows, 128),...]
where the time goes in v5:
time: 45.2 us; the launch traced here: 44.9 us
  Pallas kernels  44.1 us (98%)
  local copies, waits for them, and re-layouts  0.81 us (2%)
    pallas_call x1, Pallas kernels, body(): pl.pallas_call(kernel, out_shape=jax.ShapeDtypeStruct((GLEV, rows, 128),...  44.1 us

profile of v5, /device:TPU:30, one launch (start us, length us, event | category | flops | bytes accessed | tf_op | source)
XLA Modules:
  0.0 44.9 jit_solution(4847303694022069494)
XLA Ops:
  0.0 44.1 %shard_map.64 = f32[17,64,128]{2,1,0:T(8,128)S(1)} custom-call(bf16[136,64,128]{2,1,0:T(8,128)(2,1)} %bitcast.17, f32[136,64,128]{2,1,0:T(8,128)} %bitcast.16, f32[2,136]{1,0:T(2,128)} %modes_hbm.1, s32[8]{0:T(128)} %order_hbm.1, f32[8]{0:T(128)} %weights_hbm.1, f32[4,2048]{1,0:T(4,128)} %diff_hbm.1), custom_call_target="tpu_custom_call" | custom-call | tf_op jit(solution)/shard_map/pallas_call | solution.py:450
  44.1 0.8 %copy.11 = f32[17,4,2048]{2,1,0:T(4,128)} copy(f32[17,4,2048]{2,1,0:T(4,128)S(1)} %bitcast.15) | data formatting | bytes 1114112

commit v6 on v5

--- a/solution.py
+++ b/solution.py
@@ -14,7 +14,7 @@
 WIDE = NLON // CHUNKS
 PADDED = NLON + 256
 EXT = ROWS + 2 * DIFF
-UP = (10, 4, 7, 13)
+UP = (10, 5, 7, 12)
 FAR, NEAR, PAST = 0, 1, 2
 MSGS = CHUNKS + 1
 BY_DISTANCE = (4, 3, 5, 2, 6, 1, 7)
@@ -264,28 +264,33 @@
 
     def diffuse(n):
         lanes = pl.ds(pl.multiple_of(n * WIDE, 128), window)
-        def both_halves(c, a):
-            arm = face[c, a, :, lanes]
-            return jnp.concatenate([arm, arm], axis=0)
-
-        u = [field[a, :, lanes] for a in range(EXT)]
-        for s in range(1, DIFF + 1):
-            new = []
-            north = both_halves(1, s - 1) * (u[1] - u[0])
-            for a in range(s, EXT - s):
-                c, down = u[a - s + 1], u[a - s + 2]
-                south = both_halves(1, a) * (down - c)
-                east = both_halves(0, a) * (pltpu.roll(c, window - 1, 1) - c)
-                total = c + (south - north) + (east - pltpu.roll(east, 1, 1))
-                if a < DIFF:
-                    total = total * top_mask
-                elif a >= DIFF + ROWS:
-                    total = total * low_mask
-                new.append(total)
-                north = south
-            u = new
-        for r in range(ROWS):
-            loc[r] = weight * u[r][:, 128 : 128 + WIDE]
+        for kh in range(2):
+            ks = slice(kh * 8, kh * 8 + 8)
+            levels = [{} for _ in range(DIFF + 1)]
+            souths = [{} for _ in range(DIFF + 1)]
+
+            def cell(s, a):
+                return field[a, ks, lanes] if s == 0 else levels[s][a]
+
+            def south_of(s, a):
+                if a not in souths[s]:
+                    souths[s][a] = face[1, a, :, lanes] * (cell(s, a + 1) - cell(s, a))
+                return souths[s][a]
+
+            for t in range(1, EXT + 2 * DIFF):
+                for s in range(1, DIFF + 1):
+                    a = t - 2 * (s - 1) + (s - 1)
+                    if s <= a < EXT - s:
+                        c = cell(s - 1, a)
+                        east = face[0, a, :, lanes] * (pltpu.roll(c, window - 1, 1) - c)
+                        total = c + (south_of(s - 1, a) - south_of(s - 1, a - 1)) + (east - pltpu.roll(east, 1, 1))
+                        if a < DIFF:
+                            total = total * top_mask
+                        elif a >= DIFF + ROWS:
+                            total = total * low_mask
+                        levels[s][a] = total
+            for r in range(ROWS):
+                loc[r, ks, :] = weight * levels[DIFF][DIFF + r][:, 128 : 128 + WIDE]
         for par in range(2):
             for r in range(ROWS):
                 q = (par * ROWS + r) * MODES
@@ -363,7 +368,7 @@
             i = 1 if way == 0 else 3
             own[n, i] = both(i)
             quantize(own[n, i], zn.at[n, way], tn.at[n, way])
-        pl.when(n == 0)(lambda: start_near(n))
+        pl.when(n < 2)(lambda: start_near(n))
         own[n, 0] = both(0)
 
     def start_near(n):
@@ -403,7 +408,7 @@
         return carry
 
     lax.fori_loop(0, CHUNKS + 1, pipe, 0)
-    lax.fori_loop(1, CHUNKS, later_near, 0)
+    lax.fori_loop(2, CHUNKS, later_near, 0)
     run(stage_c)
     run(stage_d)
 

time: 45.2 us -> 44.4 us (0.982)
  Pallas kernels: 44.1 us -> 43.4 us
    pallas_call x1, Pallas kernels: 44.1 us -> 43.4 us  [body(): pl.pallas_call(kernel, out_shape=jax.ShapeDtypeStruct((GLEV, rows, 128),...]
where the time goes in v6:
time: 44.4 us; the launch traced here: 44.2 us
  Pallas kernels  43.4 us (98%)
  local copies, waits for them, and re-layouts  0.81 us (2%)
    pallas_call x1, Pallas kernels, body(): pl.pallas_call(kernel, out_shape=jax.ShapeDtypeStruct((GLEV, rows, 128),...  43.4 us

profile of v6, /device:TPU:30, one launch (start us, length us, event | category | flops | bytes accessed | tf_op | source)
XLA Modules:
  0.0 44.2 jit_solution(6047802205338908619)
XLA Ops:
  0.0 43.4 %shard_map.64 = f32[17,64,128]{2,1,0:T(8,128)S(1)} custom-call(bf16[136,64,128]{2,1,0:T(8,128)(2,1)} %bitcast.17, f32[136,64,128]{2,1,0:T(8,128)} %bitcast.16, f32[2,136]{1,0:T(2,128)} %modes_hbm.1, s32[8]{0:T(128)} %order_hbm.1, f32[8]{0:T(128)} %weights_hbm.1, f32[4,2048]{1,0:T(4,128)} %diff_hbm.1), custom_call_target="tpu_custom_call" | custom-call | tf_op jit(solution)/shard_map/pallas_call | solution.py:455
  43.4 0.8 %copy.11 = f32[17,4,2048]{2,1,0:T(4,128)} copy(f32[17,4,2048]{2,1,0:T(4,128)S(1)} %bitcast.15) | data formatting | bytes 1114112

commit v7 on v6

--- a/solution.py
+++ b/solution.py
@@ -14,7 +14,7 @@
 WIDE = NLON // CHUNKS
 PADDED = NLON + 256
 EXT = ROWS + 2 * DIFF
-UP = (10, 5, 7, 12)
+UP = (9, 5, 8, 12)
 FAR, NEAR, PAST = 0, 1, 2
 MSGS = CHUNKS + 1
 BY_DISTANCE = (4, 3, 5, 2, 6, 1, 7)

time: 44.4 us -> 44.4 us (level)
  no operation moved by 1% of the time
where the time goes in v7:
time: 44.4 us; the launch traced here: 44.1 us
  Pallas kernels  43.3 us (98%)
  local copies, waits for them, and re-layouts  0.81 us (2%)
    pallas_call x1, Pallas kernels, body(): pl.pallas_call(kernel, out_shape=jax.ShapeDtypeStruct((GLEV, rows, 128),...  43.3 us

profile of v7, /device:TPU:30, one launch (start us, length us, event | category | flops | bytes accessed | tf_op | source)
XLA Modules:
  0.0 44.1 jit_solution(7461098586818546785)
XLA Ops:
  0.0 43.3 %shard_map.64 = f32[17,64,128]{2,1,0:T(8,128)S(1)} custom-call(bf16[136,64,128]{2,1,0:T(8,128)(2,1)} %bitcast.17, f32[136,64,128]{2,1,0:T(8,128)} %bitcast.16, f32[2,136]{1,0:T(2,128)} %modes_hbm.1, s32[8]{0:T(128)} %order_hbm.1, f32[8]{0:T(128)} %weights_hbm.1, f32[4,2048]{1,0:T(4,128)} %diff_hbm.1), custom_call_target="tpu_custom_call" | custom-call | tf_op jit(solution)/shard_map/pallas_call | solution.py:455
  43.3 0.8 %copy.11 = f32[17,4,2048]{2,1,0:T(4,128)} copy(f32[17,4,2048]{2,1,0:T(4,128)S(1)} %bitcast.15) | data formatting | bytes 1114112
